TPU v7x, 128 devices: a whole 4x4x4 slice. The times are simulated.
128 devices in a mesh: eblock: 16 (over z, y), dom: 8 (over x, core).
Axes of the slice: x: 4, y: 4, z: 4, core: 2. Of those that a mesh axis runs over, the one named last changes fastest.
Arguments:
- table: bfloat16 [131072, 512], P(('eblock', 'dom')), may hold values from -1.25 to 1.25
- requests: int32 [16, 8, 8, 128], P('eblock', 'dom'), may hold values from -1 to 1023, as said below
- edge_src: int32 [16, 8, 2048], P('eblock', 'dom'), may hold values from 0 to 1023, as said below
- edge_dst: int32 [16, 8, 2048], P('eblock', 'dom'), may hold values from 0 to 1023, as said below
- labels: int32 [16, 8, 2048], P('eblock', 'dom'), may hold values 0 or 1
- neg_ids: int32 [16, 8, 128], P('eblock', 'dom'), may hold values from 0 to 1023
Outputs:
- table_grad: float32 [131072, 512], P(('eblock', 'dom'))
Inputs may be any that keep to these rules, and one draw needn't show every extreme that they name: `requests`: in each block of 128 the live entries come first and are distinct; each device has full blocks, one of them to master 8 - 1. `edge_src`: every slot names a live entry of the device's requests. `edge_dst`: every slot names a live entry of the device's requests.
All inputs are finite; a program needn't handle non-finite values. No bound on the sum of `labels` on one device may be relied on, other than what follows from the above.
Results may differ from a plain program's by a relative error of at most 0.0017.
Values may be sent and summed in bfloat16 or wider, within the bound.
A program may use at most 128 MiB of HBM per device.

v0:
```python
import jax
import jax.numpy as jnp
from jax import lax
from jax.sharding import PartitionSpec as P


def shifted(shard, axis, by):
    peers = lax.axis_size(axis)
    return lax.ppermute(shard, axis, [(i, (i + by) % peers) for i in range(peers)])


def local(table, requests, edge_src, edge_dst, labels, neg_ids):
    n_dom = lax.axis_size("dom")
    n_block = lax.axis_size("eblock")
    vcount = table.shape[0]
    width = table.shape[1]
    wanted = requests.reshape(n_dom, -1)
    asked = lax.all_to_all(wanted, "dom", split_axis=0, concat_axis=0, tiled=True)
    live = asked >= 0
    picked = jnp.where(live[..., None], table[jnp.maximum(asked, 0)], jnp.zeros((), jnp.bfloat16))
    received = lax.all_to_all(picked, "dom", split_axis=0, concat_axis=0, tiled=True)
    slot_count = received.shape[0] * received.shape[1]
    slots = received.reshape(slot_count, width)
    src_ids = edge_src.reshape(-1)
    dst_ids = edge_dst.reshape(-1)
    source = slots[src_ids]
    target = slots[dst_ids]
    pos = jnp.sum(source.astype(jnp.float32) * target.astype(jnp.float32), axis=1)
    dpos = jax.nn.sigmoid(pos) - labels.reshape(-1).astype(jnp.float32)
    own_block = table[neg_ids.reshape(-1)]
    neg_count = own_block.shape[0]
    weight = 1.0 / n_block

    def score(block, grad_acc):
        scores = lax.dot_general(
            source, block, (((1,), (1,)), ((), ())), preferred_element_type=jnp.float32
        )
        dneg = (weight * jax.nn.sigmoid(scores)).astype(jnp.bfloat16)
        grad_acc = grad_acc + jnp.dot(dneg, block, preferred_element_type=jnp.float32)
        block_grad = lax.dot_general(
            dneg, source, (((0,), (0,)), ((), ())), preferred_element_type=jnp.float32
        )
        return (grad_acc, block_grad)

    grad_start = dpos[:, None] * target.astype(jnp.float32)

    def beside_all(step, carry):
        block, grad_acc, carried = carry
        arriving = shifted(block, "eblock", 1)
        grad_acc, block_grad = score(block, grad_acc)
        carried = shifted(carried + block_grad, "eblock", 1)
        return (arriving, grad_acc, carried)

    start = (own_block, grad_start, jnp.zeros((neg_count, width), jnp.float32))
    _, grad_src, neg_grad = lax.fori_loop(0, n_block, beside_all, start)
    grad_dst = dpos[:, None] * source.astype(jnp.float32)
    slot_grad = jax.ops.segment_sum(grad_src, src_ids, slot_count) + jax.ops.segment_sum(
        grad_dst, dst_ids, slot_count
    )
    returned = lax.all_to_all(
        slot_grad.reshape(received.shape[0], received.shape[1], width),
        "dom",
        split_axis=0,
        concat_axis=0,
        tiled=True,
    )
    destination = jnp.where(live, asked, vcount).reshape(-1)
    table_grad = jax.ops.segment_sum(returned.reshape(-1, width), destination, vcount + 1)[:vcount]
    table_grad = table_grad + jax.ops.segment_sum(neg_grad, neg_ids.reshape(-1), vcount)
    return table_grad


def solution(mesh):
    return jax.shard_map(
        local,
        mesh=mesh,
        in_specs=(
            P(("eblock", "dom"), None),
            P("eblock", "dom", None, None),
            P("eblock", "dom", None),
            P("eblock", "dom", None),
            P("eblock", "dom", None),
            P("eblock", "dom", None),
        ),
        out_specs=P(("eblock", "dom"), None),
        check_vma=False,
    )
```

profile of v0, /device:TPU:0, one launch (start us, length us, event | category | flops | bytes accessed | tf_op | source)
XLA Modules:
  0.0 369.4 jit_solution(10671071384395481283)
XLA Ops:
  0.0 4.5 %all-to-all-start = ((s32[8,1,128]{2,1,0:T(1,128)}), s32[8,1,128]{2,1,0:T(1,128)S(1)}, u32[]{:S(2)}, u32[]{:S(2)}) async-start(s32[8,1,128]{2,1,0:T(1,128)} %bitcast.58), calls=%async_computation | async-start | bytes 8192 | tf_op jit(solution)/shard_map/all_to_all | solution.py:18
  9.7 4.0 %gather_fusion.1 = bf16[1024,512]{1,0:T(8,128)(2,1)S(1)} fusion(bf16[1024,512]{1,0:T(8,128)(2,1)S(1)} %copy-done, s32[1024]{0:T(1024)S(1)} %bitcast_clamp_fusion), kind=kCustom, calls=%fused_computation.1 | custom fusion | bytes 2101248 | tf_op jit(solution)/shard_map/gather | solution.py:20
  20.2 14.3 %all-to-all-done.1 = bf16[8,128,512]{2,1,0:T(8,128)(2,1)S(1)} async-done(((bf16[8,128,512]{2,1,0:T(8,128)(2,1)}), bf16[8,128,512]{2,1,0:T(8,128)(2,1)S(1)}, u32[]{:S(2)}, u32[]{:S(2)}) %all-to-all-start.1) | async-done | bytes 1048608 | tf_op jit(solution)/shard_map/all_to_all | solution.py:21
  34.5 9.2 %gather_fusion.2 = bf16[2048,512]{1,0:T(8,128)(2,1)} fusion(bf16[1024,512]{1,0:T(8,128)(2,1)S(1)} %bitcast.46, s32[2048]{0:T(1024)S(1)} %broadcast_clamp_fusion.1), kind=kCustom, calls=%fused_computation.2 | custom fusion | bytes 4202496 | tf_op jit(solution)/shard_map/gather | solution.py:26
  43.7 9.2 %gather_fusion.3 = bf16[2048,512]{1,0:T(8,128)(2,1)} fusion(bf16[1024,512]{1,0:T(8,128)(2,1)S(1)} %bitcast.47, s32[2048]{0:T(1024)S(1)} %broadcast_clamp_fusion), kind=kCustom, calls=%fused_computation.3 | custom fusion | bytes 4202496 | tf_op jit(solution)/shard_map/gather | solution.py:27
  58.2 15.0 %scatter_custom_fusion.1 = f32[1024,512]{1,0:T(8,128)} fusion(s32[2048]{0:T(1024)S(1)} %bitcast.56, bf16[2048,512]{1,0:T(8,128)(2,1)S(1)} %copy-done.1, f32[2048]{0:T(1024)S(1)} %divide_subtract_fusion, f32[]{:T(128)} %constant.13.clone.1), kind=kCustom, calls=%fused_computation.19 | custom fusion | flops 3145728 | bytes 4202500 | tf_op jit(solution)/shard_map/scatter-add | solution.py:57
  73.3 232.3 %while.14 = (s32[]{:T(128)}, bf16[128,512]{1,0:T(8,128)(2,1)}, f32[2048,512]{1,0:T(8,128)}, f32[128,512]{1,0:T(8,128)S(1)}, bf16[2048,512]{1,0:T(8,128)(2,1)S(1)}, /*index=5*/s32[]{:T(128)}) while((s32[]{:T(128)}, bf16[128,512]{1,0:T(8,128)(2,1)}, f32[2048,512]{1,0:T(8,128)}, f32[128,512]{1,0:T(8,128)S(1)}, bf16[2048,512]{1,0:T(8,128)(2,1)S(1)}, ...), condition=%wide.region_2.3_spmd, body=%wide.region_1.2_spmd.sunk | while | flops 807731200 | bytes 16777364 | solution.py:55
  79.2 4.8 %convolution_add_fusion.4 = f32[2048,512]{1,0:T(8,128)} fusion(f32[2048,512]{1,0:T(8,128)} %get-tuple-element.84, bf16[2048,128]{1,0:T(8,128)(2,1)S(1)} %fusion.33, bf16[128,512]{1,0:T(8,128)(2,1)S(1)} %copy.14), kind=kOutput, calls=%fused_computation.8.clone.1 | convolution fusion | flops 269484032 | bytes 9043968 | tf_op jit(solution)/shard_map/while/body/eval_jaxpr/dot_general | solution.py:39
  84.7 4.9 %collective-permute-done.1 = f32[128,512]{1,0:T(8,128)S(1)} collective-permute-done((f32[128,512]{1,0:T(8,128)}, f32[128,512]{1,0:T(8,128)S(1)}, u32[]{:S(2)}, u32[]{:S(2)}) %collective-permute-start.1) | collective-permute-done | bytes 262176 | tf_op jit(solution)/shard_map/while/body/eval_jaxpr/ppermute | solution.py:9
  92.4 4.8 %convolution_add_fusion.4 = f32[2048,512]{1,0:T(8,128)} fusion(f32[2048,512]{1,0:T(8,128)} %get-tuple-element.84, bf16[2048,128]{1,0:T(8,128)(2,1)S(1)} %fusion.33, bf16[128,512]{1,0:T(8,128)(2,1)S(1)} %copy.14), kind=kOutput, calls=%fused_computation.8.clone.1 | convolution fusion | flops 269484032 | bytes 9043968 | tf_op jit(solution)/shard_map/while/body/eval_jaxpr/dot_general | solution.py:39
  99.9 4.4 %collective-permute-done.1 = f32[128,512]{1,0:T(8,128)S(1)} collective-permute-done((f32[128,512]{1,0:T(8,128)}, f32[128,512]{1,0:T(8,128)S(1)}, u32[]{:S(2)}, u32[]{:S(2)}) %collective-permute-start.1) | collective-permute-done | bytes 262176 | tf_op jit(solution)/shard_map/while/body/eval_jaxpr/ppermute | solution.py:9
  107.2 4.8 %convolution_add_fusion.4 = f32[2048,512]{1,0:T(8,128)} fusion(f32[2048,512]{1,0:T(8,128)} %get-tuple-element.84, bf16[2048,128]{1,0:T(8,128)(2,1)S(1)} %fusion.33, bf16[128,512]{1,0:T(8,128)(2,1)S(1)} %copy.14), kind=kOutput, calls=%fused_computation.8.clone.1 | convolution fusion | flops 269484032 | bytes 9043968 | tf_op jit(solution)/shard_map/while/body/eval_jaxpr/dot_general | solution.py:39
  114.9 4.3 %collective-permute-done.1 = f32[128,512]{1,0:T(8,128)S(1)} collective-permute-done((f32[128,512]{1,0:T(8,128)}, f32[128,512]{1,0:T(8,128)S(1)}, u32[]{:S(2)}, u32[]{:S(2)}) %collective-permute-start.1) | collective-permute-done | bytes 262176 | tf_op jit(solution)/shard_map/while/body/eval_jaxpr/ppermute | solution.py:9
  122.0 4.8 %convolution_add_fusion.4 = f32[2048,512]{1,0:T(8,128)} fusion(f32[2048,512]{1,0:T(8,128)} %get-tuple-element.84, bf16[2048,128]{1,0:T(8,128)(2,1)S(1)} %fusion.33, bf16[128,512]{1,0:T(8,128)(2,1)S(1)} %copy.14), kind=kOutput, calls=%fused_computation.8.clone.1 | convolution fusion | flops 269484032 | bytes 9043968 | tf_op jit(solution)/shard_map/while/body/eval_jaxpr/dot_general | solution.py:39
  129.8 4.2 %collective-permute-done.1 = f32[128,512]{1,0:T(8,128)S(1)} collective-permute-done((f32[128,512]{1,0:T(8,128)}, f32[128,512]{1,0:T(8,128)S(1)}, u32[]{:S(2)}, u32[]{:S(2)}) %collective-permute-start.1) | collective-permute-done | bytes 262176 | tf_op jit(solution)/shard_map/while/body/eval_jaxpr/ppermute | solution.py:9
  136.8 4.8 %convolution_add_fusion.4 = f32[2048,512]{1,0:T(8,128)} fusion(f32[2048,512]{1,0:T(8,128)} %get-tuple-element.84, bf16[2048,128]{1,0:T(8,128)(2,1)S(1)} %fusion.33, bf16[128,512]{1,0:T(8,128)(2,1)S(1)} %copy.14), kind=kOutput, calls=%fused_computation.8.clone.1 | convolution fusion | flops 269484032 | bytes 9043968 | tf_op jit(solution)/shard_map/while/body/eval_jaxpr/dot_general | solution.py:39
  144.7 4.1 %collective-permute-done.1 = f32[128,512]{1,0:T(8,128)S(1)} collective-permute-done((f32[128,512]{1,0:T(8,128)}, f32[128,512]{1,0:T(8,128)S(1)}, u32[]{:S(2)}, u32[]{:S(2)}) %collective-permute-start.1) | collective-permute-done | bytes 262176 | tf_op jit(solution)/shard_map/while/body/eval_jaxpr/ppermute | solution.py:9
  151.6 4.8 %convolution_add_fusion.4 = f32[2048,512]{1,0:T(8,128)} fusion(f32[2048,512]{1,0:T(8,128)} %get-tuple-element.84, bf16[2048,128]{1,0:T(8,128)(2,1)S(1)} %fusion.33, bf16[128,512]{1,0:T(8,128)(2,1)S(1)} %copy.14), kind=kOutput, calls=%fused_computation.8.clone.1 | convolution fusion | flops 269484032 | bytes 9043968 | tf_op jit(solution)/shard_map/while/body/eval_jaxpr/dot_general | solution.py:39
  166.2 4.8 %convolution_add_fusion.4 = f32[2048,512]{1,0:T(8,128)} fusion(f32[2048,512]{1,0:T(8,128)} %get-tuple-element.84, bf16[2048,128]{1,0:T(8,128)(2,1)S(1)} %fusion.33, bf16[128,512]{1,0:T(8,128)(2,1)S(1)} %copy.14), kind=kOutput, calls=%fused_computation.8.clone.1 | convolution fusion | flops 269484032 | bytes 9043968 | tf_op jit(solution)/shard_map/while/body/eval_jaxpr/dot_general | solution.py:39
  180.8 4.8 %convolution_add_fusion.4 = f32[2048,512]{1,0:T(8,128)} fusion(f32[2048,512]{1,0:T(8,128)} %get-tuple-element.84, bf16[2048,128]{1,0:T(8,128)(2,1)S(1)} %fusion.33, bf16[128,512]{1,0:T(8,128)(2,1)S(1)} %copy.14), kind=kOutput, calls=%fused_computation.8.clone.1 | convolution fusion | flops 269484032 | bytes 9043968 | tf_op jit(solution)/shard_map/while/body/eval_jaxpr/dot_general | solution.py:39
  195.2 4.8 %convolution_add_fusion.4 = f32[2048,512]{1,0:T(8,128)} fusion(f32[2048,512]{1,0:T(8,128)} %get-tuple-element.84, bf16[2048,128]{1,0:T(8,128)(2,1)S(1)} %fusion.33, bf16[128,512]{1,0:T(8,128)(2,1)S(1)} %copy.14), kind=kOutput, calls=%fused_computation.8.clone.1 | convolution fusion | flops 269484032 | bytes 9043968 | tf_op jit(solution)/shard_map/while/body/eval_jaxpr/dot_general | solution.py:39
  209.5 4.8 %convolution_add_fusion.4 = f32[2048,512]{1,0:T(8,128)} fusion(f32[2048,512]{1,0:T(8,128)} %get-tuple-element.84, bf16[2048,128]{1,0:T(8,128)(2,1)S(1)} %fusion.33, bf16[128,512]{1,0:T(8,128)(2,1)S(1)} %copy.14), kind=kOutput, calls=%fused_computation.8.clone.1 | convolution fusion | flops 269484032 | bytes 9043968 | tf_op jit(solution)/shard_map/while/body/eval_jaxpr/dot_general | solution.py:39
  223.8 4.8 %convolution_add_fusion.4 = f32[2048,512]{1,0:T(8,128)} fusion(f32[2048,512]{1,0:T(8,128)} %get-tuple-element.84, bf16[2048,128]{1,0:T(8,128)(2,1)S(1)} %fusion.33, bf16[128,512]{1,0:T(8,128)(2,1)S(1)} %copy.14), kind=kOutput, calls=%fused_computation.8.clone.1 | convolution fusion | flops 269484032 | bytes 9043968 | tf_op jit(solution)/shard_map/while/body/eval_jaxpr/dot_general | solution.py:39
  238.1 4.8 %convolution_add_fusion.4 = f32[2048,512]{1,0:T(8,128)} fusion(f32[2048,512]{1,0:T(8,128)} %get-tuple-element.84, bf16[2048,128]{1,0:T(8,128)(2,1)S(1)} %fusion.33, bf16[128,512]{1,0:T(8,128)(2,1)S(1)} %copy.14), kind=kOutput, calls=%fused_computation.8.clone.1 | convolution fusion | flops 269484032 | bytes 9043968 | tf_op jit(solution)/shard_map/while/body/eval_jaxpr/dot_general | solution.py:39
  252.3 4.8 %convolution_add_fusion.4 = f32[2048,512]{1,0:T(8,128)} fusion(f32[2048,512]{1,0:T(8,128)} %get-tuple-element.84, bf16[2048,128]{1,0:T(8,128)(2,1)S(1)} %fusion.33, bf16[128,512]{1,0:T(8,128)(2,1)S(1)} %copy.14), kind=kOutput, calls=%fused_computation.8.clone.1 | convolution fusion | flops 269484032 | bytes 9043968 | tf_op jit(solution)/shard_map/while/body/eval_jaxpr/dot_general | solution.py:39
  266.4 4.8 %convolution_add_fusion.4 = f32[2048,512]{1,0:T(8,128)} fusion(f32[2048,512]{1,0:T(8,128)} %get-tuple-element.84, bf16[2048,128]{1,0:T(8,128)(2,1)S(1)} %fusion.33, bf16[128,512]{1,0:T(8,128)(2,1)S(1)} %copy.14), kind=kOutput, calls=%fused_computation.8.clone.1 | convolution fusion | flops 269484032 | bytes 9043968 | tf_op jit(solution)/shard_map/while/body/eval_jaxpr/dot_general | solution.py:39
  280.5 4.8 %convolution_add_fusion.4 = f32[2048,512]{1,0:T(8,128)} fusion(f32[2048,512]{1,0:T(8,128)} %get-tuple-element.84, bf16[2048,128]{1,0:T(8,128)(2,1)S(1)} %fusion.33, bf16[128,512]{1,0:T(8,128)(2,1)S(1)} %copy.14), kind=kOutput, calls=%fused_computation.8.clone.1 | convolution fusion | flops 269484032 | bytes 9043968 | tf_op jit(solution)/shard_map/while/body/eval_jaxpr/dot_general | solution.py:39
  294.5 4.8 %convolution_add_fusion.4 = f32[2048,512]{1,0:T(8,128)} fusion(f32[2048,512]{1,0:T(8,128)} %get-tuple-element.84, bf16[2048,128]{1,0:T(8,128)(2,1)S(1)} %fusion.33, bf16[128,512]{1,0:T(8,128)(2,1)S(1)} %copy.14), kind=kOutput, calls=%fused_computation.8.clone.1 | convolution fusion | flops 269484032 | bytes 9043968 | tf_op jit(solution)/shard_map/while/body/eval_jaxpr/dot_general | solution.py:39
  305.5 14.8 %scatter_custom_fusion = f32[1024,512]{1,0:T(8,128)} fusion(s32[2048]{0:T(1024)} %bitcast.57, f32[2048,512]{1,0:T(8,128)} %get-tuple-element.33, f32[]{:T(128)} %constant.13.clone.1), kind=kCustom, calls=%fused_computation.25 | custom fusion | flops 1048576 | bytes 2097664 | tf_op jit(solution)/shard_map/scatter-add | solution.py:57
  327.5 26.9 %all-to-all-done.2 = f32[8,128,512]{2,1,0:T(8,128)S(1)} async-done(((f32[8,128,512]{2,1,0:T(8,128)}), f32[8,128,512]{2,1,0:T(8,128)S(1)}, u32[]{:S(2)}, u32[]{:S(2)}) %all-to-all-start.2) | async-done | bytes 2097184 | tf_op jit(solution)/shard_map/all_to_all | solution.py:60
  355.7 8.0 %scatter_custom_fusion.2 = f32[1025,512]{1,0:T(8,128)S(1)} fusion(s32[1024]{0:T(1024)S(1)} %bitcast.59, f32[1024,512]{1,0:T(8,128)} %bitcast.50, f32[]{:T(128)} %constant.13.clone.1), kind=kCustom, calls=%fused_computation.22 | custom fusion | flops 524288 | bytes 2099712 | tf_op jit(solution)/shard_map/scatter-add | solution.py:68
  365.2 4.2 %scatter_fusion = f32[1024,512]{1,0:T(8,128)} fusion(f32[1024,512]{1,0:T(8,128)} %slice.12, s32[128]{0:T(128)S(1)} %bitcast.60, f32[128,512]{1,0:T(8,128)S(1)} %get-tuple-element.34), kind=kCustom, calls=%fused_computation.7 | custom fusion | flops 65536 | bytes 786944 | tf_op jit(solution)/shard_map/scatter-add | solution.py:69
  (144 shorter events, 160.3 us)
Async XLA Ops:
  14.9 19.6 %all-to-all-start.1 = ((bf16[8,128,512]{2,1,0:T(8,128)(2,1)}), bf16[8,128,512]{2,1,0:T(8,128)(2,1)S(1)}, u32[]{:S(2)}, u32[]{:S(2)}) async-start(bf16[8,128,512]{2,1,0:T(8,128)(2,1)} %broadcast_select_fusion), calls=%async_computation.1 | async-start | bytes 2097152 | tf_op jit(solution)/shard_map/all_to_all | solution.py:21
  74.2 10.5 %collective-permute-start = (bf16[128,512]{1,0:T(8,128)(2,1)S(1)}, bf16[128,512]{1,0:T(8,128)(2,1)}, u32[]{:S(2)}, u32[]{:S(2)}) collective-permute-start(bf16[128,512]{1,0:T(8,128)(2,1)S(1)} %copy.14), channel_id=1, source_target_pairs={{0,8},{8,16},{16,24},{24,32},{32,40},{40,48},{48,56},{56,64},{64,7... | collective-permute-start | bytes 393224 | tf_op jit(solution)/shard_map/while/body/eval_jaxpr/ppermute | solution.py:9
  77.7 11.9 %collective-permute-start.1 = (f32[128,512]{1,0:T(8,128)}, f32[128,512]{1,0:T(8,128)S(1)}, u32[]{:S(2)}, u32[]{:S(2)}) collective-permute-start(f32[128,512]{1,0:T(8,128)} %convolution_add_fusion.5), channel_id=1, source_target_pairs={{0,8},{8,16},{16,24},{24,32},{32,40},{40,48},{48,56},{56,64},{64,7... | collective-permute-start | bytes 786440 | tf_op jit(solution)/shard_map/while/body/eval_jaxpr/ppermute | solution.py:9
  92.4 12.0 %collective-permute-start.1 = (f32[128,512]{1,0:T(8,128)}, f32[128,512]{1,0:T(8,128)S(1)}, u32[]{:S(2)}, u32[]{:S(2)}) collective-permute-start(f32[128,512]{1,0:T(8,128)} %convolution_add_fusion.5), channel_id=1, source_target_pairs={{0,8},{8,16},{16,24},{24,32},{32,40},{40,48},{48,56},{56,64},{64,7... | collective-permute-start | bytes 786440 | tf_op jit(solution)/shard_map/while/body/eval_jaxpr/ppermute | solution.py:9
  107.2 12.0 %collective-permute-start.1 = (f32[128,512]{1,0:T(8,128)}, f32[128,512]{1,0:T(8,128)S(1)}, u32[]{:S(2)}, u32[]{:S(2)}) collective-permute-start(f32[128,512]{1,0:T(8,128)} %convolution_add_fusion.5), channel_id=1, source_target_pairs={{0,8},{8,16},{16,24},{24,32},{32,40},{40,48},{48,56},{56,64},{64,7... | collective-permute-start | bytes 786440 | tf_op jit(solution)/shard_map/while/body/eval_jaxpr/ppermute | solution.py:9
  120.1 9.7 %collective-permute-start = (bf16[128,512]{1,0:T(8,128)(2,1)S(1)}, bf16[128,512]{1,0:T(8,128)(2,1)}, u32[]{:S(2)}, u32[]{:S(2)}) collective-permute-start(bf16[128,512]{1,0:T(8,128)(2,1)S(1)} %copy.14), channel_id=1, source_target_pairs={{0,8},{8,16},{16,24},{24,32},{32,40},{40,48},{48,56},{56,64},{64,7... | collective-permute-start | bytes 393224 | tf_op jit(solution)/shard_map/while/body/eval_jaxpr/ppermute | solution.py:9
  122.0 12.0 %collective-permute-start.1 = (f32[128,512]{1,0:T(8,128)}, f32[128,512]{1,0:T(8,128)S(1)}, u32[]{:S(2)}, u32[]{:S(2)}) collective-permute-start(f32[128,512]{1,0:T(8,128)} %convolution_add_fusion.5), channel_id=1, source_target_pairs={{0,8},{8,16},{16,24},{24,32},{32,40},{40,48},{48,56},{56,64},{64,7... | collective-permute-start | bytes 786440 | tf_op jit(solution)/shard_map/while/body/eval_jaxpr/ppermute | solution.py:9
  134.9 9.8 %collective-permute-start = (bf16[128,512]{1,0:T(8,128)(2,1)S(1)}, bf16[128,512]{1,0:T(8,128)(2,1)}, u32[]{:S(2)}, u32[]{:S(2)}) collective-permute-start(bf16[128,512]{1,0:T(8,128)(2,1)S(1)} %copy.14), channel_id=1, source_target_pairs={{0,8},{8,16},{16,24},{24,32},{32,40},{40,48},{48,56},{56,64},{64,7... | collective-permute-start | bytes 393224 | tf_op jit(solution)/shard_map/while/body/eval_jaxpr/ppermute | solution.py:9
  136.8 11.9 %collective-permute-start.1 = (f32[128,512]{1,0:T(8,128)}, f32[128,512]{1,0:T(8,128)S(1)}, u32[]{:S(2)}, u32[]{:S(2)}) collective-permute-start(f32[128,512]{1,0:T(8,128)} %convolution_add_fusion.5), channel_id=1, source_target_pairs={{0,8},{8,16},{16,24},{24,32},{32,40},{40,48},{48,56},{56,64},{64,7... | collective-permute-start | bytes 786440 | tf_op jit(solution)/shard_map/while/body/eval_jaxpr/ppermute | solution.py:9
  149.7 9.8 %collective-permute-start = (bf16[128,512]{1,0:T(8,128)(2,1)S(1)}, bf16[128,512]{1,0:T(8,128)(2,1)}, u32[]{:S(2)}, u32[]{:S(2)}) collective-permute-start(bf16[128,512]{1,0:T(8,128)(2,1)S(1)} %copy.14), channel_id=1, source_target_pairs={{0,8},{8,16},{16,24},{24,32},{32,40},{40,48},{48,56},{56,64},{64,7... | collective-permute-start | bytes 393224 | tf_op jit(solution)/shard_map/while/body/eval_jaxpr/ppermute | solution.py:9
  151.6 11.8 %collective-permute-start.1 = (f32[128,512]{1,0:T(8,128)}, f32[128,512]{1,0:T(8,128)S(1)}, u32[]{:S(2)}, u32[]{:S(2)}) collective-permute-start(f32[128,512]{1,0:T(8,128)} %convolution_add_fusion.5), channel_id=1, source_target_pairs={{0,8},{8,16},{16,24},{24,32},{32,40},{40,48},{48,56},{56,64},{64,7... | collective-permute-start | bytes 786440 | tf_op jit(solution)/shard_map/while/body/eval_jaxpr/ppermute | solution.py:9
  164.3 9.8 %collective-permute-start = (bf16[128,512]{1,0:T(8,128)(2,1)S(1)}, bf16[128,512]{1,0:T(8,128)(2,1)}, u32[]{:S(2)}, u32[]{:S(2)}) collective-permute-start(bf16[128,512]{1,0:T(8,128)(2,1)S(1)} %copy.14), channel_id=1, source_target_pairs={{0,8},{8,16},{16,24},{24,32},{32,40},{40,48},{48,56},{56,64},{64,7... | collective-permute-start | bytes 393224 | tf_op jit(solution)/shard_map/while/body/eval_jaxpr/ppermute | solution.py:9
  166.2 11.7 %collective-permute-start.1 = (f32[128,512]{1,0:T(8,128)}, f32[128,512]{1,0:T(8,128)S(1)}, u32[]{:S(2)}, u32[]{:S(2)}) collective-permute-start(f32[128,512]{1,0:T(8,128)} %convolution_add_fusion.5), channel_id=1, source_target_pairs={{0,8},{8,16},{16,24},{24,32},{32,40},{40,48},{48,56},{56,64},{64,7... | collective-permute-start | bytes 786440 | tf_op jit(solution)/shard_map/while/body/eval_jaxpr/ppermute | solution.py:9
  178.8 9.7 %collective-permute-start = (bf16[128,512]{1,0:T(8,128)(2,1)S(1)}, bf16[128,512]{1,0:T(8,128)(2,1)}, u32[]{:S(2)}, u32[]{:S(2)}) collective-permute-start(bf16[128,512]{1,0:T(8,128)(2,1)S(1)} %copy.14), channel_id=1, source_target_pairs={{0,8},{8,16},{16,24},{24,32},{32,40},{40,48},{48,56},{56,64},{64,7... | collective-permute-start | bytes 393224 | tf_op jit(solution)/shard_map/while/body/eval_jaxpr/ppermute | solution.py:9
  180.8 11.6 %collective-permute-start.1 = (f32[128,512]{1,0:T(8,128)}, f32[128,512]{1,0:T(8,128)S(1)}, u32[]{:S(2)}, u32[]{:S(2)}) collective-permute-start(f32[128,512]{1,0:T(8,128)} %convolution_add_fusion.5), channel_id=1, source_target_pairs={{0,8},{8,16},{16,24},{24,32},{32,40},{40,48},{48,56},{56,64},{64,7... | collective-permute-start | bytes 786440 | tf_op jit(solution)/shard_map/while/body/eval_jaxpr/ppermute | solution.py:9
  193.2 9.7 %collective-permute-start = (bf16[128,512]{1,0:T(8,128)(2,1)S(1)}, bf16[128,512]{1,0:T(8,128)(2,1)}, u32[]{:S(2)}, u32[]{:S(2)}) collective-permute-start(bf16[128,512]{1,0:T(8,128)(2,1)S(1)} %copy.14), channel_id=1, source_target_pairs={{0,8},{8,16},{16,24},{24,32},{32,40},{40,48},{48,56},{56,64},{64,7... | collective-permute-start | bytes 393224 | tf_op jit(solution)/shard_map/while/body/eval_jaxpr/ppermute | solution.py:9
  195.2 11.5 %collective-permute-start.1 = (f32[128,512]{1,0:T(8,128)}, f32[128,512]{1,0:T(8,128)S(1)}, u32[]{:S(2)}, u32[]{:S(2)}) collective-permute-start(f32[128,512]{1,0:T(8,128)} %convolution_add_fusion.5), channel_id=1, source_target_pairs={{0,8},{8,16},{16,24},{24,32},{32,40},{40,48},{48,56},{56,64},{64,7... | collective-permute-start | bytes 786440 | tf_op jit(solution)/shard_map/while/body/eval_jaxpr/ppermute | solution.py:9
  207.6 9.7 %collective-permute-start = (bf16[128,512]{1,0:T(8,128)(2,1)S(1)}, bf16[128,512]{1,0:T(8,128)(2,1)}, u32[]{:S(2)}, u32[]{:S(2)}) collective-permute-start(bf16[128,512]{1,0:T(8,128)(2,1)S(1)} %copy.14), channel_id=1, source_target_pairs={{0,8},{8,16},{16,24},{24,32},{32,40},{40,48},{48,56},{56,64},{64,7... | collective-permute-start | bytes 393224 | tf_op jit(solution)/shard_map/while/body/eval_jaxpr/ppermute | solution.py:9
  209.5 11.5 %collective-permute-start.1 = (f32[128,512]{1,0:T(8,128)}, f32[128,512]{1,0:T(8,128)S(1)}, u32[]{:S(2)}, u32[]{:S(2)}) collective-permute-start(f32[128,512]{1,0:T(8,128)} %convolution_add_fusion.5), channel_id=1, source_target_pairs={{0,8},{8,16},{16,24},{24,32},{32,40},{40,48},{48,56},{56,64},{64,7... | collective-permute-start | bytes 786440 | tf_op jit(solution)/shard_map/while/body/eval_jaxpr/ppermute | solution.py:9
  221.9 9.7 %collective-permute-start = (bf16[128,512]{1,0:T(8,128)(2,1)S(1)}, bf16[128,512]{1,0:T(8,128)(2,1)}, u32[]{:S(2)}, u32[]{:S(2)}) collective-permute-start(bf16[128,512]{1,0:T(8,128)(2,1)S(1)} %copy.14), channel_id=1, source_target_pairs={{0,8},{8,16},{16,24},{24,32},{32,40},{40,48},{48,56},{56,64},{64,7... | collective-permute-start | bytes 393224 | tf_op jit(solution)/shard_map/while/body/eval_jaxpr/ppermute | solution.py:9
  223.8 11.4 %collective-permute-start.1 = (f32[128,512]{1,0:T(8,128)}, f32[128,512]{1,0:T(8,128)S(1)}, u32[]{:S(2)}, u32[]{:S(2)}) collective-permute-start(f32[128,512]{1,0:T(8,128)} %convolution_add_fusion.5), channel_id=1, source_target_pairs={{0,8},{8,16},{16,24},{24,32},{32,40},{40,48},{48,56},{56,64},{64,7... | collective-permute-start | bytes 786440 | tf_op jit(solution)/shard_map/while/body/eval_jaxpr/ppermute | solution.py:9
  236.2 9.7 %collective-permute-start = (bf16[128,512]{1,0:T(8,128)(2,1)S(1)}, bf16[128,512]{1,0:T(8,128)(2,1)}, u32[]{:S(2)}, u32[]{:S(2)}) collective-permute-start(bf16[128,512]{1,0:T(8,128)(2,1)S(1)} %copy.14), channel_id=1, source_target_pairs={{0,8},{8,16},{16,24},{24,32},{32,40},{40,48},{48,56},{56,64},{64,7... | collective-permute-start | bytes 393224 | tf_op jit(solution)/shard_map/while/body/eval_jaxpr/ppermute | solution.py:9
  238.1 11.4 %collective-permute-start.1 = (f32[128,512]{1,0:T(8,128)}, f32[128,512]{1,0:T(8,128)S(1)}, u32[]{:S(2)}, u32[]{:S(2)}) collective-permute-start(f32[128,512]{1,0:T(8,128)} %convolution_add_fusion.5), channel_id=1, source_target_pairs={{0,8},{8,16},{16,24},{24,32},{32,40},{40,48},{48,56},{56,64},{64,7... | collective-permute-start | bytes 786440 | tf_op jit(solution)/shard_map/while/body/eval_jaxpr/ppermute | solution.py:9
  250.4 9.7 %collective-permute-start = (bf16[128,512]{1,0:T(8,128)(2,1)S(1)}, bf16[128,512]{1,0:T(8,128)(2,1)}, u32[]{:S(2)}, u32[]{:S(2)}) collective-permute-start(bf16[128,512]{1,0:T(8,128)(2,1)S(1)} %copy.14), channel_id=1, source_target_pairs={{0,8},{8,16},{16,24},{24,32},{32,40},{40,48},{48,56},{56,64},{64,7... | collective-permute-start | bytes 393224 | tf_op jit(solution)/shard_map/while/body/eval_jaxpr/ppermute | solution.py:9
  252.3 11.3 %collective-permute-start.1 = (f32[128,512]{1,0:T(8,128)}, f32[128,512]{1,0:T(8,128)S(1)}, u32[]{:S(2)}, u32[]{:S(2)}) collective-permute-start(f32[128,512]{1,0:T(8,128)} %convolution_add_fusion.5), channel_id=1, source_target_pairs={{0,8},{8,16},{16,24},{24,32},{32,40},{40,48},{48,56},{56,64},{64,7... | collective-permute-start | bytes 786440 | tf_op jit(solution)/shard_map/while/body/eval_jaxpr/ppermute | solution.py:9
  264.5 9.8 %collective-permute-start = (bf16[128,512]{1,0:T(8,128)(2,1)S(1)}, bf16[128,512]{1,0:T(8,128)(2,1)}, u32[]{:S(2)}, u32[]{:S(2)}) collective-permute-start(bf16[128,512]{1,0:T(8,128)(2,1)S(1)} %copy.14), channel_id=1, source_target_pairs={{0,8},{8,16},{16,24},{24,32},{32,40},{40,48},{48,56},{56,64},{64,7... | collective-permute-start | bytes 393224 | tf_op jit(solution)/shard_map/while/body/eval_jaxpr/ppermute | solution.py:9
  266.4 11.2 %collective-permute-start.1 = (f32[128,512]{1,0:T(8,128)}, f32[128,512]{1,0:T(8,128)S(1)}, u32[]{:S(2)}, u32[]{:S(2)}) collective-permute-start(f32[128,512]{1,0:T(8,128)} %convolution_add_fusion.5), channel_id=1, source_target_pairs={{0,8},{8,16},{16,24},{24,32},{32,40},{40,48},{48,56},{56,64},{64,7... | collective-permute-start | bytes 786440 | tf_op jit(solution)/shard_map/while/body/eval_jaxpr/ppermute | solution.py:9
  278.6 9.8 %collective-permute-start = (bf16[128,512]{1,0:T(8,128)(2,1)S(1)}, bf16[128,512]{1,0:T(8,128)(2,1)}, u32[]{:S(2)}, u32[]{:S(2)}) collective-permute-start(bf16[128,512]{1,0:T(8,128)(2,1)S(1)} %copy.14), channel_id=1, source_target_pairs={{0,8},{8,16},{16,24},{24,32},{32,40},{40,48},{48,56},{56,64},{64,7... | collective-permute-start | bytes 393224 | tf_op jit(solution)/shard_map/while/body/eval_jaxpr/ppermute | solution.py:9
  280.5 11.2 %collective-permute-start.1 = (f32[128,512]{1,0:T(8,128)}, f32[128,512]{1,0:T(8,128)S(1)}, u32[]{:S(2)}, u32[]{:S(2)}) collective-permute-start(f32[128,512]{1,0:T(8,128)} %convolution_add_fusion.5), channel_id=1, source_target_pairs={{0,8},{8,16},{16,24},{24,32},{32,40},{40,48},{48,56},{56,64},{64,7... | collective-permute-start | bytes 786440 | tf_op jit(solution)/shard_map/while/body/eval_jaxpr/ppermute | solution.py:9
  292.6 9.8 %collective-permute-start = (bf16[128,512]{1,0:T(8,128)(2,1)S(1)}, bf16[128,512]{1,0:T(8,128)(2,1)}, u32[]{:S(2)}, u32[]{:S(2)}) collective-permute-start(bf16[128,512]{1,0:T(8,128)(2,1)S(1)} %copy.14), channel_id=1, source_target_pairs={{0,8},{8,16},{16,24},{24,32},{32,40},{40,48},{48,56},{56,64},{64,7... | collective-permute-start | bytes 393224 | tf_op jit(solution)/shard_map/while/body/eval_jaxpr/ppermute | solution.py:9
  294.5 11.1 %collective-permute-start.1 = (f32[128,512]{1,0:T(8,128)}, f32[128,512]{1,0:T(8,128)S(1)}, u32[]{:S(2)}, u32[]{:S(2)}) collective-permute-start(f32[128,512]{1,0:T(8,128)} %convolution_add_fusion.5), channel_id=1, source_target_pairs={{0,8},{8,16},{16,24},{24,32},{32,40},{40,48},{48,56},{56,64},{64,7... | collective-permute-start | bytes 786440 | tf_op jit(solution)/shard_map/while/body/eval_jaxpr/ppermute | solution.py:9
  323.7 30.7 %all-to-all-start.2 = ((f32[8,128,512]{2,1,0:T(8,128)}), f32[8,128,512]{2,1,0:T(8,128)S(1)}, u32[]{:S(2)}, u32[]{:S(2)}) async-start(f32[8,128,512]{2,1,0:T(8,128)} %bitcast.48), calls=%async_computation.2 | async-start | bytes 4194304 | tf_op jit(solution)/shard_map/all_to_all | solution.py:60
  (11 other events, 71.5 us)
where the time goes:
time: 371 us; the launch traced here: 369 us
  waiting for transfers between devices  152 us (41%)
  matrix products  108 us (29%)
  other arithmetic  53.2 us (14%)
  local copies, waits for them, and re-layouts  41.2 us (11%)
  starting transfers between devices  15.2 us (4%)
    ppermute x32, waiting for transfers between devices, shifted(): lax.ppermute(shard, axis, [(i, (i + by) % peers) for i in range(peers)])  107 us
    dot_general x16, matrix products, score(): jnp.dot(dneg, block, preferred_element_type=jnp.float32)  76.9 us
    all_to_all x1, waiting for transfers between devices, local(): lax.all_to_all(slot_grad.reshape(received.shape[0], received.shape[1], wi...  26.9 us
    dot_general x16, matrix products, score(): lax.dot_general(dneg, source, (((0,), (0,)), ((), ())), preferred_element...  19.2 us
    scatter-add x1, other arithmetic, local(): jax.ops.segment_sum(grad_dst, dst_ids, slot_count)  15 us
    scatter-add x1, other arithmetic, local(): jax.ops.segment_sum(grad_src, src_ids, slot_count)  14.8 us
    another operation x16, local copies, waits for them, and re-layouts  14.5 us
    all_to_all x1, waiting for transfers between devices, local(): lax.all_to_all(picked, 'dom', split_axis=0, concat_axis=0, tiled=True)  14.3 us
  transfers between devices with their start and end apart: 35, of which 35 were waited for; matrix products, arithmetic and copies ran while one was open for 30% of the time, Pallas kernels for 0%

commit v1 on v0

v1 whole, which is shorter than its diff:
```python
import jax
import jax.numpy as jnp
from jax import lax
from jax.experimental import pallas as pl
from jax.experimental.pallas import tpu as pltpu
from jax.sharding import PartitionSpec as P

MESH = pl.DeviceIdType.MESH
BF = jnp.bfloat16
F32 = jnp.float32
D = 512
R = 128
S = 1024
E = 2048
C = 2048
V = 1024
H = 64
LABEL = 4096.0

DOM = ((2, 0), (2, 1), (1, 0), (1, 1), (3, 0), (3, 1), (0, 1))
RING = (2, 1, 3)


def nt(a, b):
    return lax.dot_general(a, b, (((1,), (1,)), ((), ())), preferred_element_type=F32)


def nn(a, b):
    return jnp.dot(a, b, preferred_element_type=F32)


def onehot_rows(ids, count):
    column = jnp.transpose(ids)[:, :1]
    return jnp.where(lax.broadcasted_iota(jnp.int32, (R, count), 1) == column, 1.0, 0.0).astype(BF)


def onehot_columns(ids, count, base=0):
    place = lax.broadcasted_iota(jnp.int32, (count, ids.shape[1]), 0) + base
    return jnp.where(place == ids, 1.0, 0.0).astype(BF)


def rows(i, n):
    return pl.ds(pl.multiple_of(i * n, n), n)


def kernel(
    table_hbm, req_ref, src_ref, dst_ref, lab_ref, neg_ref, out_ref,
    table, reqst, asked, picked, slots, cslots, cand, dnt, st, wt, cnt, lbl, cdeg, gneg, gst, ret, xt,
    gca, gcown, rs1, part, rs2,
    tab_sem, s_req, r_req, s_slot, r_slot, s_ag1, r_ag1, s_ag2, r_ag2, s_ret, r_ret, s_rs1, r_rs1, s_rs2, r_rs2,
):
    e = lax.axis_index("eblock")
    d = lax.axis_index("dom")
    z, y = lax.div(e, 4), lax.rem(e, 4)
    x, c = lax.div(d, 2), lax.rem(d, 2)

    def plus(a, by, n=4):
        return lax.rem(a + by, n)

    def dom_peer(dx, dc):
        return plus(x, dx) * 2 + plus(c, dc, 2)

    def along(half, by):
        if half == 0:
            return (z * 4 + plus(y, by), d)
        return (plus(z, by) * 4 + y, d)

    def across(half, by):
        return along(1 - half, by)

    outer = (z, y)
    inner = (y, z)

    def remote(src, dst, ssem, rsem, to):
        return pltpu.make_async_remote_copy(
            src_ref=src, dst_ref=dst, send_sem=ssem, recv_sem=rsem, device_id=to, device_id_type=MESH
        )

    barrier = pltpu.get_barrier_semaphore()
    for dx, dc in DOM:
        pl.semaphore_signal(barrier, inc=1, device_id=(e, dom_peer(dx, dc)), device_id_type=MESH)
    for half in range(2):
        for by in RING:
            pl.semaphore_signal(barrier, inc=1, device_id=along(half, by), device_id_type=MESH)

    load = pltpu.make_async_copy(table_hbm, table, tab_sem)
    load.start()
    for p in range(8):
        reqst[p] = jnp.broadcast_to(req_ref[p : p + 1, :], (8, R))
    neg = jnp.broadcast_to(neg_ref[...], (8, R))
    neg_hot = onehot_rows(neg, V)
    pl.semaphore_wait(barrier, 13)

    req_cp = []
    for i, (dx, dc) in enumerate(DOM):
        peer = dom_peer(dx, dc)
        cp = remote(reqst.at[peer], asked.at[d], s_req.at[i], r_req.at[i], (e, peer))
        cp.start()
        req_cp.append(cp)
    asked[d] = reqst[d]

    load.wait()
    own = nn(neg_hot, table[...]).astype(BF)
    ag1 = []
    for half in range(2):
        at = rows(half * 16 + outer[half] * 4 + inner[half], H)
        cand[at, :] = own[half * H : (half + 1) * H, :]
        for i, by in enumerate(RING):
            cp = remote(cand.at[at], cand.at[at], s_ag1.at[half * 3 + i], r_ag1.at[half * 3 + i], along(half, by))
            cp.start()
            ag1.append(cp)

    for cp in req_cp:
        cp.wait_recv()
    slot_cp = []
    for dx in (2, 1, 3, 0):
        base = plus(x, dx) * 2
        hot = jnp.concatenate([onehot_rows(asked[base], V), onehot_rows(asked[base + 1], V)], axis=0)
        picked[rows(plus(x, dx), 2 * R), :] = nn(hot, table[...]).astype(BF)
        for dc in range(2):
            if (dx, dc) == (0, 0):
                continue
            i = DOM.index((dx, dc))
            peer = dom_peer(dx, dc)
            cp = remote(picked.at[rows(peer, R)], slots.at[rows(d, R)], s_slot.at[i], r_slot.at[i], (e, peer))
            cp.start()
            slot_cp.append(cp)
    slots[rows(d, R), :] = picked[rows(d, R), :]

    for cp in ag1:
        cp.wait_recv()
    ag2 = []
    for half in range(2):
        at = rows(half * 4 + outer[half], 4 * H)
        for i, by in enumerate(RING):
            cp = remote(cand.at[at], cand.at[at], s_ag2.at[half * 3 + i], r_ag2.at[half * 3 + i], across(half, by))
            cp.start()
            ag2.append(cp)

    weight = jnp.where(lab_ref[...] == 1, LABEL, 1.0)

    @pl.loop(0, 8)
    def _(t):
        at = rows(t, R)
        place = lax.broadcasted_iota(jnp.int32, (R, E), 0) + t * R
        hot = jnp.where(place == src_ref[...], 1.0, 0.0)
        st[at, :] = hot.astype(BF)
        cdeg[at, :] = jnp.broadcast_to(jnp.sum(hot, axis=1, keepdims=True), (R, R))
        wt[at, :] = jnp.where(place == dst_ref[...], weight, 0.0).astype(BF)
        xt[:, at] = onehot_columns(asked[t][:1, :], V)

    neg_cols = onehot_columns(neg_ref[...], V)
    xt[:, S : S + R] = neg_cols
    xt[:, S + R : S + 2 * R] = neg_cols

    @pl.loop(0, 16)
    def _(t):
        a = rows(lax.div(t, 4), 256)
        b = rows(lax.rem(t, 4), 256)
        one = nt(st[a, :], wt[b, :])
        two = nt(wt[a, :], st[b, :])
        ones = jnp.floor(one * (1.0 / LABEL)) + jnp.floor(two * (1.0 / LABEL))
        lbl[a, b] = ones
        cnt[a, b] = one + two - (LABEL - 1.0) * ones

    for cp in ag2:
        cp.wait_recv()
    for dx in (0, 1, 3, 2):
        for dc in range(2):
            if (dx, dc) != (0, 0):
                slot_cp[DOM.index((dx, dc))].wait_recv()
        q = plus(x, 4 - dx)
        at = rows(q, 256)
        cslots[at, :] = (slots[at, :].astype(F32) * cdeg[at, :1]).astype(BF)

        @pl.loop(0, 4)
        def _(t):
            block = rows(t, 512)
            there = nt(slots[at, :], cand[block, :])
            dneg = (jnp.tanh(there * 0.5) * (1.0 / 32) + (1.0 / 32)).astype(BF)
            more = nn(dneg, cand[block, :])

            @pl.when(t == 0)
            def _():
                gneg[at, :] = more

            @pl.when(t > 0)
            def _():
                gneg[at, :] += more

            turned = nt(cand[block, :], slots[at, :])
            dnt[block, at] = (jnp.tanh(turned * 0.5) * (1.0 / 32) + (1.0 / 32)).astype(BF)

    ret_cp = []
    rs_cp = []

    def slot_grads(dx):
        q = plus(x, dx)
        at = rows(q, 256)
        gneg[at, :] = gneg[at, :] * cdeg[at, :1]

        @pl.loop(0, 4)
        def _(t):
            block = rows(t, 256)
            pos = nt(slots[at, :], slots[block, :])
            w = cnt[at, block] * (jnp.tanh(pos * 0.5) * 0.5 + 0.5) - lbl[at, block]
            gneg[at, :] += nn(w.astype(BF), slots[block, :])

        gst[at, :] = gneg[at, :].astype(BF)
        for dc in range(2):
            if (dx, dc) == (0, 0):
                ret[rows(d, R), :] = gst[rows(d, R), :]
                continue
            i = DOM.index((dx, dc))
            peer = dom_peer(dx, dc)
            cp = remote(gst.at[rows(peer, R)], ret.at[rows(d, R)], s_ret.at[i], r_ret.at[i], (e, peer))
            cp.start()
            ret_cp.append(cp)

    def cand_grads(by):
        for half in range(2):
            at = rows(half * 4 + plus(outer[half], by), 4 * H)
            total = nn(dnt[at, :], cslots[...])
            if by == 0:
                gcown[half] = total
            else:
                i = half * 3 + RING.index(by)
                gca[i] = total.astype(BF)
                cp = remote(gca.at[i], rs1.at[i], s_rs1.at[i], r_rs1.at[i], across(half, by))
                cp.start()
                rs_cp.append(cp)

    for by in (2, 1, 3, 0):
        slot_grads(by)
        cand_grads(by)

    for cp in rs_cp:
        cp.wait_recv()
    rs2_cp = []
    for half in range(2):
        total = gcown[half]
        for i in range(3):
            total = total + rs1[half * 3 + i].astype(F32)
        part[half] = total
        for i, by in enumerate(RING):
            k = half * 3 + i
            cp = remote(
                part.at[half, rows(plus(inner[half], by), H)], rs2.at[k], s_rs2.at[k], r_rs2.at[k], along(half, by)
            )
            cp.start()
            rs2_cp.append(cp)
    for cp in ret_cp:
        cp.wait_recv()
    for cp in rs2_cp:
        cp.wait_recv()
    for half in range(2):
        total = part[half, rows(inner[half], H), :]
        for i in range(3):
            total = total + rs2[half * 3 + i]
        high = total.astype(BF)
        ret[S + half * H : S + (half + 1) * H, :] = high
        ret[S + R + half * H : S + R + (half + 1) * H, :] = (total - high.astype(F32)).astype(BF)

    @pl.loop(0, 4)
    def _(t):
        at = rows(t, 256)
        out_ref[at, :] = nn(xt[at, :], ret[...])

    for cp in req_cp + ag1 + ag2 + slot_cp + ret_cp + rs_cp + rs2_cp:
        cp.wait_send()


def local(table, requests, edge_src, edge_dst, labels, neg_ids):
    vmem = pl.BlockSpec(memory_space=pltpu.VMEM)
    dma = pltpu.SemaphoreType.DMA
    return pl.pallas_call(
        kernel,
        out_shape=jax.ShapeDtypeStruct((V, D), F32),
        in_specs=[pl.BlockSpec(memory_space=pl.ANY)] + [vmem] * 5,
        out_specs=vmem,
        scratch_shapes=[
            pltpu.VMEM((V, D), BF),
            pltpu.VMEM((8, 8, R), jnp.int32),
            pltpu.VMEM((8, 8, R), jnp.int32),
            pltpu.VMEM((S, D), BF),
            pltpu.VMEM((S, D), BF),
            pltpu.VMEM((S, D), BF),
            pltpu.VMEM((C, D), BF),
            pltpu.VMEM((C, S), BF),
            pltpu.VMEM((S, E), BF),
            pltpu.VMEM((S, E), BF),
            pltpu.VMEM((S, S), F32),
            pltpu.VMEM((S, S), F32),
            pltpu.VMEM((S, R), F32),
            pltpu.VMEM((S, D), F32),
            pltpu.VMEM((S, D), BF),
            pltpu.VMEM((S + 2 * R, D), BF),
            pltpu.VMEM((V, S + 2 * R), BF),
            pltpu.VMEM((6, 4 * H, D), BF),
            pltpu.VMEM((2, 4 * H, D), F32),
            pltpu.VMEM((6, 4 * H, D), BF),
            pltpu.VMEM((2, 4 * H, D), F32),
            pltpu.VMEM((6, H, D), F32),
            dma,
            dma((7,)), dma((7,)),
            dma((7,)), dma((7,)),
            dma((6,)), dma((6,)),
            dma((6,)), dma((6,)),
            dma((7,)), dma((7,)),
            dma((6,)), dma((6,)),
            dma((6,)), dma((6,)),
        ],
        compiler_params=pltpu.CompilerParams(
            collective_id=0, has_side_effects=True, vmem_limit_bytes=56 * 1024 * 1024
        ),
        name="link_step",
    )(
        table,
        requests.reshape(8, R),
        edge_src.reshape(1, E),
        edge_dst.reshape(1, E),
        labels.reshape(1, E),
        neg_ids.reshape(1, R),
    )


def solution(mesh):
    return jax.shard_map(
        local,
        mesh=mesh,
        in_specs=(
            P(("eblock", "dom"), None),
            P("eblock", "dom", None, None),
            P("eblock", "dom", None),
            P("eblock", "dom", None),
            P("eblock", "dom", None),
            P("eblock", "dom", None),
        ),
        out_specs=P(("eblock", "dom"), None),
        check_vma=False,
    )
```

time: 371 us -> 77.4 us (0.21)
  waiting for transfers between devices: 152 us -> 0 us
  matrix products: 108 us -> 0 us
  Pallas kernels: 0 us -> 73.3 us
  other arithmetic: 53.2 us -> 0 us
  local copies, waits for them, and re-layouts: 41.2 us -> 3.08 us
  starting transfers between devices: 15.2 us -> 0 us
    dot_general x48 -> x0, matrix products: 108 us -> none  [the longest x16 76.9 us: score(): jnp.dot(dneg, block, preferred_element_type=jnp.float32)]
    ppermute x32 -> x0, waiting for transfers between devices: 107 us -> none  [shifted(): lax.ppermute(shard, axis, [(i, (i + by) % peers) for i in range(peers)])]
    pallas_call x0 -> x1, Pallas kernels: none -> 73.3 us  [local(): pl.pallas_call(kernel, out_shape=jax.ShapeDtypeStruct((V, D), F32), in_sp...]
    all_to_all x3 -> x0, waiting for transfers between devices: 45.1 us -> none  [the longest x1 26.9 us: local(): lax.all_to_all(slot_grad.reshape(received.shape[0], received.shape[1], wi...]
    scatter-add x4 -> x0, other arithmetic: 42 us -> none  [the longest x1 15 us: local(): jax.ops.segment_sum(grad_dst, dst_ids, slot_count)]
    gather x4 -> x0, local copies, waits for them, and re-layouts: 23.9 us -> none  [the longest x1 9.2 us: local(): source = slots[src_ids]]
    another operation x16 -> x0, local copies, waits for them, and re-layouts: 14.5 us -> none
    all_to_all x3 -> x0, starting transfers between devices: 12 us -> none  [the longest x1 4.51 us: local(): lax.all_to_all(wanted, 'dom', split_axis=0, concat_axis=0, tiled=True)]
  transfers between devices with their start and end apart: 35 -> 0, of which waited for: 35 -> 0; matrix products, arithmetic and copies ran while one was open for 30% -> 0% of each run, Pallas kernels for 0% -> 0%
where the time goes in v1:
time: 77.4 us; the launch traced here: 76.4 us
  Pallas kernels  73.3 us (95%)
  local copies, waits for them, and re-layouts  3.08 us (4%)
    pallas_call x1, Pallas kernels, local(): pl.pallas_call(kernel, out_shape=jax.ShapeDtypeStruct((V, D), F32), in_sp...  73.3 us
    unnamed x1, local copies, waits for them, and re-layouts  3.08 us

profile of v1, /device:TPU:0, one launch (start us, length us, event | category | flops | bytes accessed | tf_op | source)
XLA Modules:
  0.0 76.4 jit_solution(6148651333112223413)
XLA Ops:
  0.0 73.3 %link_step.1 = f32[1024,512]{1,0:T(8,128)} custom-call(bf16[1024,512]{1,0:T(8,128)(2,1)} %table_hbm.1, s32[8,128]{1,0:T(8,128)} %bitcast.8, s32[1,2048]{1,0:T(1,128)} %bitcast.5, s32[1,2048]{1,0:T(1,128)} %bitcast.6, s32[1,2048]{1,0:T(1,128)} %bitcast.7, s32[1,128]{1,0:T(1,128)} %bitcast.9), custom_call_target="tpu_custom_call" | custom-call | tf_op jit(solution)/shard_map/link_step/pallas_call | solution.py:276
  73.4 3.1 %copy.8 = f32[1024,512]{1,0:T(8,128)} copy(f32[1024,512]{1,0:T(8,128)} %link_step.1) | data formatting | bytes 4194304

commit v2 on v1

v2 whole, which is shorter than its diff:
```python
import jax
import jax.numpy as jnp
from jax import lax
from jax.experimental import pallas as pl
from jax.experimental.pallas import tpu as pltpu
from jax.sharding import PartitionSpec as P

MESH = pl.DeviceIdType.MESH
BF = jnp.bfloat16
F32 = jnp.float32
D = 512
R = 128
S = 1024
E = 2048
C = 2048
V = 1024
H = 64
LABEL = 4096.0

DOM = ((2, 0), (2, 1), (1, 0), (1, 1), (3, 0), (3, 1), (0, 1))
RING = (2, 1, 3)


def nt(a, b):
    return lax.dot_general(a, b, (((1,), (1,)), ((), ())), preferred_element_type=F32)


def nn(a, b):
    return jnp.dot(a, b, preferred_element_type=F32)


def onehot_rows(ids, count):
    column = jnp.transpose(ids)[:, :1]
    return jnp.where(lax.broadcasted_iota(jnp.int32, (R, count), 1) == column, 1.0, 0.0).astype(BF)


def onehot_columns(ids, count, base=0):
    place = lax.broadcasted_iota(jnp.int32, (count, ids.shape[1]), 0) + base
    return jnp.where(place == ids, 1.0, 0.0).astype(BF)


def rows(i, n):
    return pl.ds(pl.multiple_of(i * n, n), n)


def step_kernel(
    table_hbm, req_ref, src_ref, dst_ref, lab_ref, neg_ref, ret, asked_out, neg_out,
    table, reqst, asked, picked, slots, cslots, cand, dnt, st, wt, cnt, off, cdeg, selfw, gneg, gst,
    opp, side, kept, gcown, rly, rs1, part, rs2,
    tab_sem, own_sem, s_req, r_req, s_slot, r_slot, s_ag1, r_ag1, s_ag2, r_ag2, s_ret, r_ret, s_rs1, r_rs1, s_rs2, r_rs2,
):
    e = lax.axis_index("eblock")
    d = lax.axis_index("dom")
    z, y = lax.div(e, 4), lax.rem(e, 4)
    x, c = lax.div(d, 2), lax.rem(d, 2)

    def plus(a, by, n=4):
        return lax.rem(a + by, n)

    def dom_peer(dx, dc):
        return plus(x, dx) * 2 + plus(c, dc, 2)

    def along(half, by):
        if half == 0:
            return (z * 4 + plus(y, by), d)
        return (plus(z, by) * 4 + y, d)

    def across(half, by):
        return along(1 - half, by)

    outer = (z, y)
    inner = (y, z)

    def group(half, by, first=0, count=4 * H):
        start = (half * 4 + plus(outer[half], by)) * (4 * H) + first
        return pl.ds(pl.multiple_of(start, count), count)

    def remote(src, dst, ssem, rsem, to):
        return pltpu.make_async_remote_copy(
            src_ref=src, dst_ref=dst, send_sem=ssem, recv_sem=rsem, device_id=to, device_id_type=MESH
        )

    barrier = pltpu.get_barrier_semaphore()
    for dx, dc in DOM:
        pl.semaphore_signal(barrier, inc=1, device_id=(e, dom_peer(dx, dc)), device_id_type=MESH)
    for half in range(2):
        for by in RING:
            pl.semaphore_signal(barrier, inc=1, device_id=along(half, by), device_id_type=MESH)

    load = pltpu.make_async_copy(table_hbm, table, tab_sem)
    load.start()
    for p in range(8):
        reqst[p] = jnp.broadcast_to(req_ref[p : p + 1, :], (8, R))
    neg_hot = onehot_rows(jnp.broadcast_to(neg_ref[...], (8, R)), V)
    pl.semaphore_wait(barrier, 13)

    req_cp = []
    for i, (dx, dc) in enumerate(DOM):
        peer = dom_peer(dx, dc)
        cp = remote(reqst.at[peer], asked.at[d], s_req.at[i], r_req.at[i], (e, peer))
        cp.start()
        req_cp.append(cp)
    asked[d] = reqst[d]

    load.wait()
    own = (nn(neg_hot, table[...]) * 0.5).astype(BF)
    ag1 = []
    for half in range(2):
        at = rows(half * 16 + outer[half] * 4 + inner[half], H)
        cand[at, :] = own[half * H : (half + 1) * H, :]
        for i, by in enumerate(RING):
            cp = remote(cand.at[at], cand.at[at], s_ag1.at[half * 3 + i], r_ag1.at[half * 3 + i], along(half, by))
            cp.start()
            ag1.append(cp)

    slot_cp = [None] * 7
    for dx in (2, 1, 3, 0):
        for dc in range(2):
            if (dx, dc) != (0, 0):
                req_cp[DOM.index((dx, dc))].wait_recv()
    for dx in (2, 1, 3, 0):
        base = plus(x, dx) * 2
        hot = jnp.concatenate([onehot_rows(asked[base], V), onehot_rows(asked[base + 1], V)], axis=0)
        picked[rows(plus(x, dx), 2 * R), :] = nn(hot, table[...]).astype(BF)
        for dc in range(2):
            if (dx, dc) == (0, 0):
                continue
            i = DOM.index((dx, dc))
            peer = dom_peer(dx, dc)
            cp = remote(picked.at[rows(peer, R)], slots.at[rows(d, R)], s_slot.at[i], r_slot.at[i], (e, peer))
            cp.start()
            slot_cp[i] = cp
    slots[rows(d, R), :] = picked[rows(d, R), :]

    for cp in ag1:
        cp.wait_recv()
    ag2 = {}

    def gather_step(half, k, to, by, first):
        at = group(half, by, first, 2 * H)
        cp = remote(cand.at[at], cand.at[at], s_ag2.at[half * 6 + k], r_ag2.at[half * 6 + k], across(half, to))
        cp.start()
        ag2[half, k] = cp

    for half in range(2):
        gather_step(half, 0, 1, 0, 0)
        gather_step(half, 1, 3, 0, 2 * H)
    for half in range(2):
        gather_step(half, 2, 1, 0, 2 * H)
        gather_step(half, 3, 3, 0, 0)

    weight = jnp.where(lab_ref[...] == 1, LABEL, 1.0)

    @pl.loop(0, 8)
    def _(t):
        at = rows(t, R)
        place = lax.broadcasted_iota(jnp.int32, (R, E), 0) + t * R
        one = jnp.where(place == src_ref[...], 1.0, 0.0)
        two = jnp.where(place == dst_ref[...], 1.0, 0.0)
        both = one + two
        heavy = both * weight
        st[at, :] = both.astype(BF)
        wt[at, :] = heavy.astype(BF)
        cdeg[at, :] = jnp.broadcast_to(jnp.sum(one, axis=1, keepdims=True), (R, R))
        selfw[at, :] = jnp.broadcast_to(jnp.sum(one * two * weight, axis=1, keepdims=True), (R, R))

    def pair_counts(t):
        at = rows(t, 256)
        full = nt(st[at, :], wt[...])
        ones = jnp.floor(full * (1.0 / LABEL))
        many = full * 0.5 - (0.5 * LABEL - 0.5) * ones
        cnt[at, :] = many
        off[at, :] = many - ones
        alone = selfw[at, :1]
        ones = jnp.floor(alone * (1.0 / LABEL))
        many = alone - (LABEL - 1.0) * ones
        same = lax.broadcasted_iota(jnp.int32, (256, 256), 0) == lax.broadcasted_iota(jnp.int32, (256, 256), 1)
        cnt[at, at] = jnp.where(same, many, cnt[at, at])
        off[at, at] = jnp.where(same, many - 2.0 * ones, off[at, at])

    pl.loop(0, 2)(pair_counts)

    for half in range(2):
        ag2[half, 0].wait_recv()
        gather_step(half, 4, 1, 3, 0)
        ag2[half, 1].wait_recv()
        gather_step(half, 5, 3, 1, 2 * H)

    pl.loop(2, 4)(pair_counts)

    for half in range(2):
        for k in range(2, 6):
            ag2[half, k].wait_recv()
    for dx in (0, 2, 3, 1):
        for dc in range(2):
            if (dx, dc) != (0, 0):
                slot_cp[DOM.index((dx, dc))].wait_recv()
        at = rows(plus(x, 4 - dx), 256)
        cslots[at, :] = (slots[at, :].astype(F32) * (cdeg[at, :1] * (1.0 / 32))).astype(BF)
        dneg = (jnp.tanh(nt(slots[at, :], cand[...])) + 1.0).astype(BF)
        gneg[at, :] = nn(dneg, cand[...])
        dnt[:, at] = jnp.transpose(dneg)

    ret_cp = []
    rs_cp = {}

    def slot_grads(dx):
        at = rows(plus(x, dx), 256)
        pos = nt(slots[at, :] * jnp.asarray(0.5, BF), slots[...])
        w = (cnt[at, :] * jnp.tanh(pos) + off[at, :]).astype(BF)
        gst[at, :] = (gneg[at, :] * (cdeg[at, :1] * (1.0 / 16)) + nn(w, slots[...])).astype(BF)
        for dc in range(2):
            if (dx, dc) == (0, 0):
                cp = pltpu.make_async_copy(gst.at[rows(d, R)], ret.at[rows(d, R)], own_sem)
                cp.start()
                own_cp.append(cp)
                continue
            i = DOM.index((dx, dc))
            peer = dom_peer(dx, dc)
            cp = remote(gst.at[rows(peer, R)], ret.at[rows(d, R)], s_ret.at[i], r_ret.at[i], (e, peer))
            cp.start()
            ret_cp.append(cp)

    own_cp = []

    def reduce_step(half, k, src, dst, to):
        cp = remote(src, dst, s_rs1.at[half * 6 + k], r_rs1.at[half * 6 + k], across(half, to))
        cp.start()
        rs_cp[half, k] = cp

    lo, hi = pl.ds(0, 2 * H), pl.ds(2 * H, 2 * H)
    sides = ((1, lo, hi, 0), (3, hi, lo, 1))

    for half in range(2):
        opp[half] = nn(dnt[group(half, 2), :], cslots[...]).astype(BF)
        reduce_step(half, 0, opp.at[half, lo], rly.at[half * 2], 1)
        reduce_step(half, 1, opp.at[half, hi], rly.at[half * 2 + 1], 3)
    slot_grads(2)
    for half in range(2):
        for by, late, early, s in sides:
            n = half * 2 + s
            total = nn(dnt[group(half, by), :], cslots[...])
            side[n] = total.astype(BF)
            kept[n] = total[2 * H * s : 2 * H * (s + 1), :]
            reduce_step(half, 2 + s, side.at[n, early], rs1.at[n, early], by)
    slot_grads(1)
    slot_grads(3)
    for half in range(2):
        for by, late, early, s in sides:
            n = half * 2 + s
            rs_cp[half, s].wait_recv()
            side[n, late, :] = (kept[n] + rly[n].astype(F32)).astype(BF)
            reduce_step(half, 4 + s, side.at[n, late], rs1.at[n, late], by)
    for half in range(2):
        gcown[half] = nn(dnt[group(half, 0), :], cslots[...])
    slot_grads(0)

    for half in range(2):
        for k in range(2, 6):
            rs_cp[half, k].wait_recv()
    rs2_cp = []
    for half in range(2):
        part[half] = gcown[half] + rs1[half * 2].astype(F32) + rs1[half * 2 + 1].astype(F32)
        for i, by in enumerate(RING):
            k = half * 3 + i
            cp = remote(
                part.at[half, rows(plus(inner[half], by), H)], rs2.at[k], s_rs2.at[k], r_rs2.at[k], along(half, by)
            )
            cp.start()
            rs2_cp.append(cp)
    asked_out[...] = asked[...]
    for cp in ret_cp:
        cp.wait_recv()
    for cp in rs2_cp:
        cp.wait_recv()
    for half in range(2):
        total = part[half, rows(inner[half], H), :]
        for i in range(3):
            total = total + rs2[half * 3 + i]
        neg_out[half * H : (half + 1) * H, :] = total

    own_cp[0].wait()
    for cp in req_cp + ag1 + list(ag2.values()) + slot_cp + ret_cp + list(rs_cp.values()) + rs2_cp:
        cp.wait_send()


def scatter_kernel(ret, asked, neg_ref, neg, out_ref):
    base = pl.program_id(0) * 256
    hot = jnp.concatenate([onehot_columns(asked[p, :1, :], 256, base) for p in range(8)], axis=1)
    cols = onehot_columns(neg_ref[...], 256, base)
    high = neg[...].astype(BF)
    low = (neg[...] - high.astype(F32)).astype(BF)
    out_ref[...] = nn(hot, ret[...]) + nn(cols, high) + nn(cols, low)


def local(table, requests, edge_src, edge_dst, labels, neg_ids):
    vmem = pl.BlockSpec(memory_space=pltpu.VMEM)
    hbm = pl.BlockSpec(memory_space=pl.ANY)
    dma = pltpu.SemaphoreType.DMA
    negs = neg_ids.reshape(1, R)
    ret, asked, neg = pl.pallas_call(
        step_kernel,
        out_shape=(
            jax.ShapeDtypeStruct((S, D), BF),
            jax.ShapeDtypeStruct((8, 8, R), jnp.int32),
            jax.ShapeDtypeStruct((R, D), F32),
        ),
        in_specs=[hbm] + [vmem] * 5,
        out_specs=(hbm, vmem, vmem),
        scratch_shapes=[
            pltpu.VMEM((V, D), BF),
            pltpu.VMEM((8, 8, R), jnp.int32),
            pltpu.VMEM((8, 8, R), jnp.int32),
            pltpu.VMEM((S, D), BF),
            pltpu.VMEM((S, D), BF),
            pltpu.VMEM((S, D), BF),
            pltpu.VMEM((C, D), BF),
            pltpu.VMEM((C, S), BF),
            pltpu.VMEM((S, E), BF),
            pltpu.VMEM((S, E), BF),
            pltpu.VMEM((S, S), F32),
            pltpu.VMEM((S, S), F32),
            pltpu.VMEM((S, R), F32),
            pltpu.VMEM((S, R), F32),
            pltpu.VMEM((S, D), F32),
            pltpu.VMEM((S, D), BF),
            pltpu.VMEM((2, 4 * H, D), BF),
            pltpu.VMEM((4, 4 * H, D), BF),
            pltpu.VMEM((4, 2 * H, D), F32),
            pltpu.VMEM((2, 4 * H, D), F32),
            pltpu.VMEM((4, 2 * H, D), BF),
            pltpu.VMEM((4, 4 * H, D), BF),
            pltpu.VMEM((2, 4 * H, D), F32),
            pltpu.VMEM((6, H, D), F32),
            dma, dma,
            dma((7,)), dma((7,)),
            dma((7,)), dma((7,)),
            dma((6,)), dma((6,)),
            dma((12,)), dma((12,)),
            dma((7,)), dma((7,)),
            dma((12,)), dma((12,)),
            dma((6,)), dma((6,)),
        ],
        compiler_params=pltpu.CompilerParams(
            collective_id=0, has_side_effects=True, vmem_limit_bytes=56 * 1024 * 1024
        ),
        name="link_step",
    )(
        table,
        requests.reshape(8, R),
        edge_src.reshape(1, E),
        edge_dst.reshape(1, E),
        labels.reshape(1, E),
        negs,
    )
    whole = lambda shape: pl.BlockSpec(shape, lambda i: (0,) * len(shape))
    return pl.pallas_call(
        scatter_kernel,
        grid=(V // 256,),
        out_shape=jax.ShapeDtypeStruct((V, D), F32),
        in_specs=[whole((S, D)), whole((8, 8, R)), whole((1, R)), whole((R, D))],
        out_specs=pl.BlockSpec((256, D), lambda i: (i, 0)),
        compiler_params=pltpu.CompilerParams(vmem_limit_bytes=24 * 1024 * 1024),
        name="scatter",
    )(ret, asked, negs, neg)


def solution(mesh):
    return jax.shard_map(
        local,
        mesh=mesh,
        in_specs=(
            P(("eblock", "dom"), None),
            P("eblock", "dom", None, None),
            P("eblock", "dom", None),
            P("eblock", "dom", None),
            P("eblock", "dom", None),
            P("eblock", "dom", None),
        ),
        out_specs=P(("eblock", "dom"), None),
        check_vma=False,
    )
```

time: 77.4 us -> 59.9 us (0.77)
  the two profiles are of different devices: /device:TPU:0 before, /device:TPU:1 now
where the time goes in v2:
time: 59.9 us; the launch traced here: 59.6 us
  Pallas kernels  56 us (93%)
  local copies, waits for them, and re-layouts  3.58 us (6%)
    pallas_call x1, Pallas kernels, local(): pl.pallas_call(step_kernel, out_shape=(jax.ShapeDtypeStruct((S, D), BF),...  52.7 us
    unnamed x8, local copies, waits for them, and re-layouts  3.58 us
    pallas_call x1, Pallas kernels, local(): pl.pallas_call(scatter_kernel, grid=(V // 256,), out_shape=jax.ShapeDtype...  3.29 us

profile of v2, /device:TPU:1, one launch (start us, length us, event | category | flops | bytes accessed | tf_op | source)
XLA Modules:
  0.0 59.6 jit_solution(1943384393762886612)
XLA Ops:
  0.0 52.7 %link_step.1 = (bf16[1024,512]{1,0:T(8,128)(2,1)}, s32[8,8,128]{2,1,0:T(8,128)}, f32[128,512]{1,0:T(8,128)}) custom-call(bf16[1024,512]{1,0:T(8,128)(2,1)} %table_hbm.1, s32[8,128]{1,0:T(8,128)} %bitcast.10, s32[1,2048]{1,0:T(1,128)} %bitcast.7, s32[1,2048]{1,0:T(1,128)} %bitcast.8, s32[1,2048]{1,0:T(1,128)} %bitcast.9, s32[1,128]{1,0:T(1,128)} %bitcast.5), custom_call_target="tpu_custom_call" | custom-call | tf_op jit(solution)/shard_map/link_step/pallas_call | solution.py:301
  52.7 0.0 copy-start
  52.7 1.2 %copy-done = bf16[1024,512]{1,0:T(8,128)(2,1)S(1)} copy-done((bf16[1024,512]{1,0:T(8,128)(2,1)S(1)}, bf16[1024,512]{1,0:T(8,128)(2,1)}, u32[]{:S(2)}) %copy-start) | copy-done | bytes 1048600
  53.9 0.0 copy-start.1
  53.9 0.9 %copy-done.1 = f32[128,512]{1,0:T(8,128)S(1)} copy-done((f32[128,512]{1,0:T(8,128)S(1)}, f32[128,512]{1,0:T(8,128)}, u32[]{:S(2)}) %copy-start.1) | copy-done | bytes 262168
  54.9 0.0 copy-start.2
  54.9 0.8 %copy-done.2 = s32[8,8,128]{2,1,0:T(8,128)S(1)} copy-done((s32[8,8,128]{2,1,0:T(8,128)S(1)}, s32[8,8,128]{2,1,0:T(8,128)}, u32[]{:S(2)}) %copy-start.2) | copy-done | bytes 32792
  55.6 0.0 copy-start.3
  55.6 0.7 %copy-done.3 = s32[1,1,128]{2,1,0:T(1,128)S(1)} copy-done((s32[1,1,128]{2,1,0:T(1,128)S(1)}, s32[1,1,128]{2,1,0:T(1,128)}, u32[]{:S(2)}) %copy-start.3) | copy-done | bytes 536
  56.3 3.3 %scatter.1 = f32[1024,512]{1,0:T(8,128)} custom-call(bf16[1024,512]{1,0:T(8,128)(2,1)S(1)} %copy-done, s32[8,8,128]{2,1,0:T(8,128)S(1)} %copy-done.2, s32[1,128]{1,0:T(1,128)S(1)} %bitcast.6, f32[128,512]{1,0:T(8,128)S(1)} %copy-done.1), custom_call_target="tpu_custom_call" | custom-call | tf_op jit(solution)/shard_map/scatter/pallas_call | solution.py:357
Async XLA Ops:
  52.7 1.2 %copy-start = (bf16[1024,512]{1,0:T(8,128)(2,1)S(1)}, bf16[1024,512]{1,0:T(8,128)(2,1)}, u32[]{:S(2)}) copy-start(bf16[1024,512]{1,0:T(8,128)(2,1)} %get-tuple-element.8.ret) | copy-start | bytes 3145732
  53.9 0.9 %copy-start.1 = (f32[128,512]{1,0:T(8,128)S(1)}, f32[128,512]{1,0:T(8,128)}, u32[]{:S(2)}) copy-start(f32[128,512]{1,0:T(8,128)} %get-tuple-element.10.neg) | copy-start | bytes 786436
  54.9 0.8 %copy-start.2 = (s32[8,8,128]{2,1,0:T(8,128)S(1)}, s32[8,8,128]{2,1,0:T(8,128)}, u32[]{:S(2)}) copy-start(s32[8,8,128]{2,1,0:T(8,128)} %get-tuple-element.9.asked) | copy-start | bytes 98308
  55.6 0.7 %copy-start.3 = (s32[1,1,128]{2,1,0:T(1,128)S(1)}, s32[1,1,128]{2,1,0:T(1,128)}, u32[]{:S(2)}) copy-start(s32[1,1,128]{2,1,0:T(1,128)} %param.11) | copy-start | bytes 1540

commit v3 on v2

v3 whole, which is shorter than its diff:
```python
import jax
import jax.numpy as jnp
from jax import lax
from jax.experimental import pallas as pl
from jax.experimental.pallas import tpu as pltpu
from jax.sharding import PartitionSpec as P

MESH = pl.DeviceIdType.MESH
BF = jnp.bfloat16
F32 = jnp.float32
D = 512
R = 128
S = 1024
E = 2048
C = 2048
V = 1024
H = 64
G = 4 * H
LABEL = 4096.0

DOM = ((1, 0), (1, 1), (3, 0), (3, 1), (2, 0), (2, 1), (0, 1))
RING = (2, 1, 3)
ORDER = (0, 1, 3, 2)


def nt(a, b):
    return lax.dot_general(a, b, (((1,), (1,)), ((), ())), preferred_element_type=F32)


def nn(a, b):
    return jnp.dot(a, b, preferred_element_type=F32)


def onehot_rows(ids, count):
    column = jnp.transpose(ids)[:, :1]
    return jnp.where(lax.broadcasted_iota(jnp.int32, (R, count), 1) == column, 1.0, 0.0).astype(BF)


def onehot_columns(ids, count, base=0):
    place = lax.broadcasted_iota(jnp.int32, (count, ids.shape[1]), 0) + base
    return jnp.where(place == ids, 1.0, 0.0).astype(BF)


def rows(i, n):
    return pl.ds(pl.multiple_of(i * n, n), n)


def chunk(dx, dc):
    return pl.ds((dx * 2 + dc) * R, R)


def pair(dx):
    return pl.ds(dx * 2 * R, 2 * R)


def group(half, by, first=0, count=G):
    return pl.ds((ORDER.index(by) * 2 + half) * G + first, count)


def step_kernel(
    table_hbm, req_hbm, src_hbm, dst_hbm, lab_hbm, neg_hbm, ret, asked_out, rs2, part_out,
    table, req, src, dst, lab, neg, reqst, asked, picked, slots, cslots, cand, dnt, st, wt, cnt, off, cdeg, selfw,
    gneg, gst, opp, side, kept, gcown, rly, rs1, part, part_bf,
    in_sem, out_sem, s_req, r_req, s_slot, r_slot, s_ag1, r_ag1, s_ag2, r_ag2, s_ret, r_ret, s_rs1, r_rs1, s_rs2, r_rs2,
):
    e = lax.axis_index("eblock")
    d = lax.axis_index("dom")
    z, y = lax.div(e, 4), lax.rem(e, 4)
    x, c = lax.div(d, 2), lax.rem(d, 2)

    def plus(a, by, n=4):
        return lax.rem(a + by, n)

    def dom_peer(dx, dc):
        return plus(x, dx) * 2 + plus(c, dc, 2)

    def along(half, by):
        if half == 0:
            return (z * 4 + plus(y, by), d)
        return (plus(z, by) * 4 + y, d)

    def across(half, by):
        return along(1 - half, by)

    def remote(src, dst, ssem, rsem, to):
        return pltpu.make_async_remote_copy(
            src_ref=src, dst_ref=dst, send_sem=ssem, recv_sem=rsem, device_id=to, device_id_type=MESH
        )

    def local_copy(src, dst, sem):
        cp = pltpu.make_async_copy(src, dst, sem)
        cp.start()
        return cp

    barrier = pltpu.get_barrier_semaphore()
    for dx, dc in ((2, 0), (2, 1), (1, 0), (1, 1), (3, 0), (3, 1), (0, 1)):
        pl.semaphore_signal(barrier, inc=1, device_id=(e, dom_peer(dx, dc)), device_id_type=MESH)
    for by in RING:
        for half in range(2):
            pl.semaphore_signal(barrier, inc=1, device_id=along(half, by), device_id_type=MESH)

    loads = [
        local_copy(a, b, in_sem.at[i])
        for i, (a, b) in enumerate(
            ((req_hbm, req), (neg_hbm, neg), (table_hbm, table), (src_hbm, src), (dst_hbm, dst), (lab_hbm, lab))
        )
    ]
    loads[0].wait()
    for p in range(8):
        reqst[p] = jnp.broadcast_to(req[p : p + 1, :], (8, R))
    loads[1].wait()
    neg_hot = onehot_rows(jnp.broadcast_to(neg[...], (8, R)), V)
    pl.semaphore_wait(barrier, 13)

    req_cp = {}
    for i, (dx, dc) in enumerate(((2, 0), (2, 1), (1, 0), (1, 1), (3, 0), (3, 1), (0, 1))):
        peer = dom_peer(dx, dc)
        cp = remote(reqst.at[peer], asked.at[(4 - dx) % 4 * 2 + dc], s_req.at[i], r_req.at[i], (e, peer))
        cp.start()
        req_cp[dx, dc] = cp
    asked[0] = reqst[d]

    loads[2].wait()
    own = (nn(neg_hot, table[...]) * 0.5).astype(BF)
    ag1 = {}
    ag2 = {}

    def gather_step(half, k, to, by, first, count):
        cp = remote(
            cand.at[group(half, by, first, count)], cand.at[group(half, (by - to) % 4, first, count)],
            s_ag2.at[half * 10 + k], r_ag2.at[half * 10 + k], across(half, to),
        )
        cp.start()
        ag2[half, k] = cp

    for half in range(2):
        cand[group(half, 0, 0, H), :] = own[half * H : (half + 1) * H, :]
    for by in RING:
        for half in range(2):
            k = half * 3 + RING.index(by)
            place = group(half, 0, ORDER.index((4 - by) % 4) * H, H)
            cp = remote(cand.at[group(half, 0, 0, H)], cand.at[place], s_ag1.at[k], r_ag1.at[k], along(half, by))
            cp.start()
            ag1[half, by] = cp
    for half in range(2):
        gather_step(half, 0, 1, 0, 0, H)
        gather_step(half, 1, 3, 0, 0, H)

    for cp in loads[3:]:
        cp.wait()
    weight = jnp.where(lab[...] == 1, LABEL, 1.0)

    @pl.loop(0, 8)
    def _(t):
        at = rows(t, R)
        first = dom_peer(lax.div(t, 2), lax.rem(t, 2)) * R
        place = lax.broadcasted_iota(jnp.int32, (R, E), 0) + first
        one = jnp.where(place == src[...], 1.0, 0.0)
        two = jnp.where(place == dst[...], 1.0, 0.0)
        both = one + two
        st[at, :] = both.astype(BF)
        wt[at, :] = (both * weight).astype(BF)
        cdeg[at, :] = jnp.broadcast_to(jnp.sum(one, axis=1, keepdims=True), (R, R))
        selfw[at, :] = jnp.broadcast_to(jnp.sum(one * two * weight, axis=1, keepdims=True), (R, R))

    for cp in req_cp.values():
        cp.wait_recv()
    slot_cp = {}
    for dx in (1, 3, 2, 0):
        hot = jnp.concatenate([onehot_rows(asked[dx * 2], V), onehot_rows(asked[dx * 2 + 1], V)], axis=0)
        rows_out = nn(hot, table[...]).astype(BF)
        if dx == 0:
            slots[chunk(0, 0), :] = rows_out[:R, :]
            picked[chunk(0, 1), :] = rows_out[R:, :]
        else:
            picked[pair(dx), :] = rows_out
        for dc in range(2):
            if (dx, dc) == (0, 0):
                continue
            i = DOM.index((dx, dc))
            cp = remote(
                picked.at[chunk(dx, dc)], slots.at[chunk((4 - dx) % 4, dc)],
                s_slot.at[i], r_slot.at[i], (e, dom_peer(dx, dc)),
            )
            cp.start()
            slot_cp[dx, dc] = cp
    asked_cp = local_copy(asked, asked_out, out_sem.at[0])

    for cp in ag1.values():
        cp.wait_recv()
    for half in range(2):
        gather_step(half, 2, 1, 0, H, 96)
        gather_step(half, 3, 3, 0, H + 96, 96)
    for half in range(2):
        gather_step(half, 4, 1, 0, H + 96, 96)
        gather_step(half, 5, 3, 0, H, 96)
    for half in range(2):
        ag2[half, 0].wait_recv()
        gather_step(half, 6, 1, 3, 0, H // 2)
        ag2[half, 1].wait_recv()
        gather_step(half, 7, 3, 1, H // 2, H // 2)

    def pair_counts(t):
        at = rows(t, 256)
        full = nt(st[at, :], wt[...])
        ones = jnp.floor(full * (1.0 / LABEL))
        many = full * 0.5 - (0.5 * LABEL - 0.5) * ones
        cnt[at, :] = many
        off[at, :] = many - ones
        alone = selfw[at, :1]
        ones = jnp.floor(alone * (1.0 / LABEL))
        many = alone - (LABEL - 1.0) * ones
        same = lax.broadcasted_iota(jnp.int32, (256, 256), 0) == lax.broadcasted_iota(jnp.int32, (256, 256), 1)
        cnt[at, at] = jnp.where(same, many, cnt[at, at])
        off[at, at] = jnp.where(same, many - 2.0 * ones, off[at, at])

    pl.loop(0, 3)(pair_counts)

    for half in range(2):
        ag2[half, 2].wait_recv()
        gather_step(half, 8, 1, 3, H, 96)
        ag2[half, 3].wait_recv()
        gather_step(half, 9, 3, 1, H + 96, 96)

    pl.loop(3, 4)(pair_counts)

    for half in range(2):
        for k in range(4, 10):
            ag2[half, k].wait_recv()
    lost = jnp.zeros((1, D), F32)
    for dx in (0, 1, 3, 2):
        for dc in range(2):
            if (dx, dc) != (0, 0):
                slot_cp[(4 - dx) % 4, dc].wait_recv()
        at = pair(dx)
        many = slots[at, :].astype(F32) * (cdeg[at, :1] * (1.0 / 32))
        kept_many = many.astype(BF)
        cslots[at, :] = kept_many
        lost = lost + jnp.sum(many - kept_many.astype(F32), axis=0, keepdims=True)
        dneg = (jnp.tanh(nt(slots[at, :], cand[...])) + 1.0).astype(BF)
        gneg[at, :] = nn(dneg, cand[...])
        dnt[:, at] = jnp.transpose(dneg)

    ret_cp = []
    rs_cp = {}

    def slot_grads(dx):
        at = pair(dx)
        pos = nt(slots[at, :] * jnp.asarray(0.5, BF), slots[...])
        w = (cnt[at, :] * jnp.tanh(pos) + off[at, :]).astype(BF)
        gst[at, :] = (gneg[at, :] * (cdeg[at, :1] * (1.0 / 16)) + nn(w, slots[...])).astype(BF)
        for dc in range(2):
            if (dx, dc) == (0, 0):
                continue
            i = DOM.index((dx, dc))
            cp = remote(
                gst.at[chunk(dx, dc)], ret.at[chunk((4 - dx) % 4, dc)],
                s_ret.at[i], r_ret.at[i], (e, dom_peer(dx, dc)),
            )
            cp.start()
            ret_cp.append(cp)

    def cand_grads(half, by):
        return nn(dnt[group(half, by), :], cslots[...]) + lost

    def reduce_step(half, k, src, dst, to):
        cp = remote(src, dst, s_rs1.at[half * 6 + k], r_rs1.at[half * 6 + k], across(half, to))
        cp.start()
        rs_cp[half, k] = cp

    lo, hi = pl.ds(0, 2 * H), pl.ds(2 * H, 2 * H)
    sides = ((1, lo, hi, 0), (3, hi, lo, 1))

    def opposite(half):
        opp[half] = cand_grads(half, 2).astype(BF)
        reduce_step(half, 0, opp.at[half, lo], rly.at[half * 2], 1)
        reduce_step(half, 1, opp.at[half, hi], rly.at[half * 2 + 1], 3)

    def neighbours_early(half):
        for by, late, early, s in sides:
            n = half * 2 + s
            total = cand_grads(half, by)
            side[n] = total.astype(BF)
            kept[n] = total[2 * H * s : 2 * H * (s + 1), :]
            reduce_step(half, 2 + s, side.at[n, early], rs1.at[n, early], by)

    def neighbours_late(half):
        for by, late, early, s in sides:
            n = half * 2 + s
            rs_cp[half, s].wait_recv()
            side[n, late, :] = (kept[n] + rly[n].astype(F32)).astype(BF)
            reduce_step(half, 4 + s, side.at[n, late], rs1.at[n, late], by)

    def own_group(half):
        gcown[half] = cand_grads(half, 0)

    opposite(0)
    opposite(1)
    slot_grads(1)
    neighbours_early(0)
    neighbours_early(1)
    slot_grads(3)
    slot_grads(2)
    neighbours_late(0)
    neighbours_late(1)
    own_group(0)
    own_group(1)
    slot_grads(0)
    own_cp = local_copy(gst.at[chunk(0, 0)], ret.at[chunk(0, 0)], out_sem.at[1])

    rs2_cp = []
    for half in range(2):
        for k in range(2, 6):
            rs_cp[half, k].wait_recv()
        total = gcown[half] + rs1[half * 2].astype(F32) + rs1[half * 2 + 1].astype(F32)
        part[half] = total[:H, :]
        part_bf[half] = total.astype(BF)
        for by in RING:
            k = half * 3 + RING.index(by)
            cp = remote(
                part_bf.at[half, pl.ds(ORDER.index(by) * H, H)], rs2.at[pl.ds(k * H, H)],
                s_rs2.at[k], r_rs2.at[k], along(half, by),
            )
            cp.start()
            rs2_cp.append(cp)
    part_cp = local_copy(part, part_out, out_sem.at[2])
    for cp in ret_cp:
        cp.wait_recv()
    for cp in rs2_cp:
        cp.wait_recv()

    for cp in (asked_cp, own_cp, part_cp):
        cp.wait()
    for cps in (req_cp, ag1, ag2, slot_cp, rs_cp):
        for cp in cps.values():
            cp.wait_send()
    for cp in ret_cp + rs2_cp:
        cp.wait_send()


def scatter_kernel(
    ret_hbm, asked_hbm, neg_hbm, rs2_hbm, part_hbm, out_hbm, ret, asked, neg, rs2, part, out, in_sem, out_sem
):
    pairs = ((asked_hbm, asked), (ret_hbm, ret.at[pl.ds(0, S)]), (neg_hbm, neg), (rs2_hbm, rs2), (part_hbm, part))
    loads = []
    for i, (a, b) in enumerate(pairs):
        cp = pltpu.make_async_copy(a, b, in_sem.at[i])
        cp.start()
        loads.append(cp)
    loads[0].wait()
    loads[2].wait()
    hots = []
    for t in range(4):
        hots.append(
            jnp.concatenate(
                [onehot_columns(asked[p, :1, :], 256, t * 256) for p in range(8)]
                + [onehot_columns(neg[...], 256, t * 256)] * 2,
                axis=1,
            )
        )
    loads[3].wait()
    loads[4].wait()
    for half in range(2):
        total = part[half]
        for i in range(3):
            k = half * 3 + i
            total = total + rs2[k * H : (k + 1) * H, :].astype(F32)
        high = total.astype(BF)
        ret[S + half * H : S + (half + 1) * H, :] = high
        ret[S + R + half * H : S + R + (half + 1) * H, :] = (total - high.astype(F32)).astype(BF)
    loads[1].wait()
    stores = []
    for t in range(4):
        at = pl.ds(t * 256, 256)
        out[at, :] = nn(hots[t], ret[...])
        cp = pltpu.make_async_copy(out.at[at], out_hbm.at[at], out_sem.at[t])
        cp.start()
        stores.append(cp)
    for cp in stores:
        cp.wait()


def local(table, requests, edge_src, edge_dst, labels, neg_ids):
    hbm = pl.BlockSpec(memory_space=pltpu.HBM)
    dma = pltpu.SemaphoreType.DMA
    negs = neg_ids.reshape(1, R)
    ids = pltpu.VMEM((1, E), jnp.int32)
    ret, asked, rs2, part = pl.pallas_call(
        step_kernel,
        out_shape=(
            jax.ShapeDtypeStruct((S, D), BF),
            jax.ShapeDtypeStruct((8, 8, R), jnp.int32),
            jax.ShapeDtypeStruct((6 * H, D), BF),
            jax.ShapeDtypeStruct((2, H, D), F32),
        ),
        in_specs=[hbm] * 6,
        out_specs=(hbm,) * 4,
        scratch_shapes=[
            pltpu.VMEM((V, D), BF),
            pltpu.VMEM((8, R), jnp.int32),
            ids, ids, ids,
            pltpu.VMEM((1, R), jnp.int32),
            pltpu.VMEM((8, 8, R), jnp.int32),
            pltpu.VMEM((8, 8, R), jnp.int32),
            pltpu.VMEM((S, D), BF),
            pltpu.VMEM((S, D), BF),
            pltpu.VMEM((S, D), BF),
            pltpu.VMEM((C, D), BF),
            pltpu.VMEM((C, S), BF),
            pltpu.VMEM((S, E), BF),
            pltpu.VMEM((S, E), BF),
            pltpu.VMEM((S, S), F32),
            pltpu.VMEM((S, S), F32),
            pltpu.VMEM((S, R), F32),
            pltpu.VMEM((S, R), F32),
            pltpu.VMEM((S, D), F32),
            pltpu.VMEM((S, D), BF),
            pltpu.VMEM((2, G, D), BF),
            pltpu.VMEM((4, G, D), BF),
            pltpu.VMEM((4, 2 * H, D), F32),
            pltpu.VMEM((2, G, D), F32),
            pltpu.VMEM((4, 2 * H, D), BF),
            pltpu.VMEM((4, G, D), BF),
            pltpu.VMEM((2, H, D), F32),
            pltpu.VMEM((2, G, D), BF),
            dma((6,)), dma((3,)),
            dma((7,)), dma((7,)),
            dma((7,)), dma((7,)),
            dma((6,)), dma((6,)),
            dma((20,)), dma((20,)),
            dma((7,)), dma((7,)),
            dma((12,)), dma((12,)),
            dma((6,)), dma((6,)),
        ],
        compiler_params=pltpu.CompilerParams(
            collective_id=0, has_side_effects=True, vmem_limit_bytes=56 * 1024 * 1024
        ),
        name="link_step",
    )(
        table,
        requests.reshape(8, R),
        edge_src.reshape(1, E),
        edge_dst.reshape(1, E),
        labels.reshape(1, E),
        negs,
    )
    return pl.pallas_call(
        scatter_kernel,
        out_shape=jax.ShapeDtypeStruct((V, D), F32),
        in_specs=[hbm] * 5,
        out_specs=hbm,
        scratch_shapes=[
            pltpu.VMEM((S + 2 * R, D), BF),
            pltpu.VMEM((8, 8, R), jnp.int32),
            pltpu.VMEM((1, R), jnp.int32),
            pltpu.VMEM((6 * H, D), BF),
            pltpu.VMEM((2, H, D), F32),
            pltpu.VMEM((V, D), F32),
            dma((5,)), dma((4,)),
        ],
        compiler_params=pltpu.CompilerParams(vmem_limit_bytes=56 * 1024 * 1024),
        name="scatter",
    )(ret, asked, negs, rs2, part)


def solution(mesh):
    return jax.shard_map(
        local,
        mesh=mesh,
        in_specs=(
            P(("eblock", "dom"), None),
            P("eblock", "dom", None, None),
            P("eblock", "dom", None),
            P("eblock", "dom", None),
            P("eblock", "dom", None),
            P("eblock", "dom", None),
        ),
        out_specs=P(("eblock", "dom"), None),
        check_vma=False,
    )
```

time: 59.9 us -> 50.1 us (0.84)
  the two profiles are of different devices: /device:TPU:1 before, /device:TPU:0 now
where the time goes in v3:
time: 50.1 us; the launch traced here: 50 us
  Pallas kernels  49.8 us (99%)
    pallas_call x1, Pallas kernels, local(): pl.pallas_call(step_kernel, out_shape=(jax.ShapeDtypeStruct((S, D), BF),...  45.8 us
    pallas_call x1, Pallas kernels, local(): pl.pallas_call(scatter_kernel, out_shape=jax.ShapeDtypeStruct((V, D), F32...  4.07 us

profile of v3, /device:TPU:0, one launch (start us, length us, event | category | flops | bytes accessed | tf_op | source)
XLA Modules:
  0.0 50.0 jit_solution(1249757452987266990)
XLA Ops:
  0.0 45.8 %link_step.1 = (bf16[1024,512]{1,0:T(8,128)(2,1)}, s32[8,8,128]{2,1,0:T(8,128)}, bf16[384,512]{1,0:T(8,128)(2,1)}, f32[2,64,512]{2,1,0:T(8,128)}) custom-call(bf16[1024,512]{1,0:T(8,128)(2,1)} %table_hbm.1, s32[8,128]{1,0:T(8,128)} %bitcast.8, s32[1,2048]{1,0:T(1,128)} %bitcast.5, s32[1,2048]{1,0:T(1,128)} %bitcast.6, s32[1,2048]{1,0:T(1,128)} %bitcast.7, ...), custom_call_target="tpu_custom_call" | custom-call | tf_op jit(solution)/shard_map/link_step/pallas_call | solution.py:388
  45.8 4.1 %scatter.1 = f32[1024,512]{1,0:T(8,128)} custom-call(bf16[1024,512]{1,0:T(8,128)(2,1)} %get-tuple-element.9.ret_hbm, s32[8,8,128]{2,1,0:T(8,128)} %get-tuple-element.10.asked_hbm, s32[1,128]{1,0:T(1,128)} %bitcast.10, bf16[384,512]{1,0:T(8,128)(2,1)} %get-tuple-element.11.rs2_hbm, f32[2,64,512]{2,1,0:T(8,128)} %get-tuple-element.12.part_hbm), custom_call_target="tpu_custom_call" | custom-call | tf_op jit(solution)/shard_map/scatter/pallas_call | solution.py:447

commit v4 on v3

--- a/solution.py
+++ b/solution.py
@@ -59,7 +59,7 @@
 
 def step_kernel(
     table_hbm, req_hbm, src_hbm, dst_hbm, lab_hbm, neg_hbm, ret, asked_out, rs2, part_out,
-    table, req, src, dst, lab, neg, reqst, asked, picked, slots, cslots, cand, dnt, st, wt, cnt, off, cdeg, selfw,
+    table, req, src, dst, lab, neg, reqst, asked, picked, slots, cslots, cand, dnt, st, wt, cnt, off, cdeg,
     gneg, gst, opp, side, kept, gcown, rly, rs1, part, part_bf,
     in_sem, out_sem, s_req, r_req, s_slot, r_slot, s_ag1, r_ag1, s_ag2, r_ag2, s_ret, r_ret, s_rs1, r_rs1, s_rs2, r_rs2,
 ):
@@ -128,40 +128,53 @@
     def gather_step(half, k, to, by, first, count):
         cp = remote(
             cand.at[group(half, by, first, count)], cand.at[group(half, (by - to) % 4, first, count)],
-            s_ag2.at[half * 10 + k], r_ag2.at[half * 10 + k], across(half, to),
+            s_ag2.at[half * 14 + k], r_ag2.at[half * 14 + k], across(half, to),
         )
         cp.start()
         ag2[half, k] = cp
 
     for half in range(2):
         cand[group(half, 0, 0, H), :] = own[half * H : (half + 1) * H, :]
-    for by in RING:
+    def short_step(by):
         for half in range(2):
             k = half * 3 + RING.index(by)
             place = group(half, 0, ORDER.index((4 - by) % 4) * H, H)
             cp = remote(cand.at[group(half, 0, 0, H)], cand.at[place], s_ag1.at[k], r_ag1.at[k], along(half, by))
             cp.start()
             ag1[half, by] = cp
+
+    short_step(1)
+    short_step(3)
     for half in range(2):
         gather_step(half, 0, 1, 0, 0, H)
         gather_step(half, 1, 3, 0, 0, H)
+    short_step(2)
 
     for cp in loads[3:]:
         cp.wait()
     weight = jnp.where(lab[...] == 1, LABEL, 1.0)
-
-    @pl.loop(0, 8)
-    def _(t):
+    line = lax.broadcasted_iota(jnp.int32, (R, E), 0)
+    loop_weight = jnp.where(src[...] == dst[...], weight, 0.0)
+    sums = jnp.where(line == 0, 1.0, jnp.where(line == 1, loop_weight, 0.0)).astype(BF)
+    weight = weight.astype(BF)
+    line = line.astype(F32).astype(BF)
+
+    def incidence(t):
         at = rows(t, R)
         first = dom_peer(lax.div(t, 2), lax.rem(t, 2)) * R
-        place = lax.broadcasted_iota(jnp.int32, (R, E), 0) + first
-        one = jnp.where(place == src[...], 1.0, 0.0)
-        two = jnp.where(place == dst[...], 1.0, 0.0)
-        both = one + two
+
+        def ends(ids):
+            place = ids[...] - first
+            place = jnp.where((place >= 0) & (place < R), place, R).astype(F32).astype(BF)
+            return jnp.where(line == place, jnp.ones((R, E), BF), jnp.zeros((R, E), BF))
+
+        one = ends(src)
+        both = one + ends(dst)
         st[at, :] = both.astype(BF)
         wt[at, :] = (both * weight).astype(BF)
-        cdeg[at, :] = jnp.broadcast_to(jnp.sum(one, axis=1, keepdims=True), (R, R))
-        selfw[at, :] = jnp.broadcast_to(jnp.sum(one * two * weight, axis=1, keepdims=True), (R, R))
+        cdeg[at, :] = nt(one, sums)
+
+    pl.loop(0, 4)(incidence)
 
     for cp in req_cp.values():
         cp.wait_recv()
@@ -186,19 +199,25 @@
             slot_cp[dx, dc] = cp
     asked_cp = local_copy(asked, asked_out, out_sem.at[0])
 
-    for cp in ag1.values():
-        cp.wait_recv()
-    for half in range(2):
-        gather_step(half, 2, 1, 0, H, 96)
-        gather_step(half, 3, 3, 0, H + 96, 96)
-    for half in range(2):
-        gather_step(half, 4, 1, 0, H + 96, 96)
-        gather_step(half, 5, 3, 0, H, 96)
+    for half in range(2):
+        for by in (1, 3):
+            ag1[half, by].wait_recv()
+    for half in range(2):
+        gather_step(half, 2, 1, 0, H, H)
+        gather_step(half, 3, 3, 0, 2 * H, H)
+    for half in range(2):
+        gather_step(half, 4, 1, 0, 2 * H, H)
+        gather_step(half, 5, 3, 0, H, H)
     for half in range(2):
         ag2[half, 0].wait_recv()
-        gather_step(half, 6, 1, 3, 0, H // 2)
+        gather_step(half, 8, 1, 3, 0, H // 2)
         ag2[half, 1].wait_recv()
-        gather_step(half, 7, 3, 1, H // 2, H // 2)
+        gather_step(half, 9, 3, 1, H // 2, H // 2)
+    pl.loop(4, 8)(incidence)
+    for half in range(2):
+        ag1[half, 2].wait_recv()
+        gather_step(half, 6, 1, 0, 3 * H, H)
+        gather_step(half, 7, 3, 0, 3 * H, H)
 
     def pair_counts(t):
         at = rows(t, 256)
@@ -207,28 +226,36 @@
         many = full * 0.5 - (0.5 * LABEL - 0.5) * ones
         cnt[at, :] = many
         off[at, :] = many - ones
-        alone = selfw[at, :1]
+        alone = cdeg[at, 1:2]
         ones = jnp.floor(alone * (1.0 / LABEL))
         many = alone - (LABEL - 1.0) * ones
         same = lax.broadcasted_iota(jnp.int32, (256, 256), 0) == lax.broadcasted_iota(jnp.int32, (256, 256), 1)
         cnt[at, at] = jnp.where(same, many, cnt[at, at])
         off[at, at] = jnp.where(same, many - 2.0 * ones, off[at, at])
 
-    pl.loop(0, 3)(pair_counts)
+    pl.loop(0, 1)(pair_counts)
 
     for half in range(2):
         ag2[half, 2].wait_recv()
-        gather_step(half, 8, 1, 3, H, 96)
+        gather_step(half, 10, 1, 3, H, H)
         ag2[half, 3].wait_recv()
-        gather_step(half, 9, 3, 1, H + 96, 96)
-
+        gather_step(half, 11, 3, 1, 2 * H, H)
+
+    pl.loop(1, 3)(pair_counts)
+    for half in range(2):
+        ag2[half, 6].wait_recv()
+        gather_step(half, 12, 1, 3, 3 * H, H // 2)
+        ag2[half, 7].wait_recv()
+        gather_step(half, 13, 3, 1, 3 * H + H // 2, H // 2)
     pl.loop(3, 4)(pair_counts)
 
     for half in range(2):
-        for k in range(4, 10):
+        for k in (4, 5):
             ag2[half, k].wait_recv()
+    near, far = pl.ds(0, 6 * G), pl.ds(6 * G, 2 * G)
     lost = jnp.zeros((1, D), F32)
-    for dx in (0, 1, 3, 2):
+
+    def arrive(dx, lost):
         for dc in range(2):
             if (dx, dc) != (0, 0):
                 slot_cp[(4 - dx) % 4, dc].wait_recv()
@@ -236,10 +263,25 @@
         many = slots[at, :].astype(F32) * (cdeg[at, :1] * (1.0 / 32))
         kept_many = many.astype(BF)
         cslots[at, :] = kept_many
-        lost = lost + jnp.sum(many - kept_many.astype(F32), axis=0, keepdims=True)
-        dneg = (jnp.tanh(nt(slots[at, :], cand[...])) + 1.0).astype(BF)
-        gneg[at, :] = nn(dneg, cand[...])
-        dnt[:, at] = jnp.transpose(dneg)
+        return lost + jnp.sum(many - kept_many.astype(F32), axis=0, keepdims=True)
+
+    def score(dx, block, add):
+        at = pair(dx)
+        dneg = (jnp.tanh(nt(slots[at, :], cand[block, :])) + 1.0).astype(BF)
+        more = nn(dneg, cand[block, :])
+        gneg[at, :] = gneg[at, :] + more if add else more
+        dnt[block, at] = jnp.transpose(dneg)
+
+    for dx in (0, 1, 3, 2)[:3]:
+        lost = arrive(dx, lost)
+        score(dx, near, False)
+    for half in range(2):
+        for k in range(8, 14):
+            ag2[half, k].wait_recv()
+    for dx in (0, 1, 3, 2)[:3]:
+        score(dx, far, True)
+    lost = arrive((0, 1, 3, 2)[3], lost)
+    score((0, 1, 3, 2)[3], pl.ds(0, C), False)
 
     ret_cp = []
     rs_cp = {}
@@ -296,11 +338,11 @@
 
     opposite(0)
     opposite(1)
-    slot_grads(1)
+    slot_grads(2)
     neighbours_early(0)
     neighbours_early(1)
+    slot_grads(1)
     slot_grads(3)
-    slot_grads(2)
     neighbours_late(0)
     neighbours_late(1)
     own_group(0)
@@ -349,15 +391,13 @@
         loads.append(cp)
     loads[0].wait()
     loads[2].wait()
-    hots = []
-    for t in range(4):
-        hots.append(
-            jnp.concatenate(
-                [onehot_columns(asked[p, :1, :], 256, t * 256) for p in range(8)]
-                + [onehot_columns(neg[...], 256, t * 256)] * 2,
-                axis=1,
-            )
-        )
+    line = lax.broadcasted_iota(jnp.int32, (256, R), 0).astype(F32).astype(BF)
+
+    def hot(ids, first):
+        place = ids - first
+        place = jnp.where((place >= 0) & (place < 256), place, 256).astype(F32).astype(BF)
+        return jnp.where(line == place, jnp.ones((256, R), BF), jnp.zeros((256, R), BF))
+
     loads[3].wait()
     loads[4].wait()
     for half in range(2):
@@ -372,7 +412,9 @@
     stores = []
     for t in range(4):
         at = pl.ds(t * 256, 256)
-        out[at, :] = nn(hots[t], ret[...])
+        negs = hot(neg[...], t * 256)
+        hots = jnp.concatenate([hot(asked[p, :1, :], t * 256) for p in range(8)] + [negs, negs], axis=1)
+        out[at, :] = nn(hots, ret[...])
         cp = pltpu.make_async_copy(out.at[at], out_hbm.at[at], out_sem.at[t])
         cp.start()
         stores.append(cp)
@@ -412,7 +454,6 @@
             pltpu.VMEM((S, S), F32),
             pltpu.VMEM((S, S), F32),
             pltpu.VMEM((S, R), F32),
-            pltpu.VMEM((S, R), F32),
             pltpu.VMEM((S, D), F32),
             pltpu.VMEM((S, D), BF),
             pltpu.VMEM((2, G, D), BF),
@@ -427,7 +468,7 @@
             dma((7,)), dma((7,)),
             dma((7,)), dma((7,)),
             dma((6,)), dma((6,)),
-            dma((20,)), dma((20,)),
+            dma((28,)), dma((28,)),
             dma((7,)), dma((7,)),
             dma((12,)), dma((12,)),
             dma((6,)), dma((6,)),

time: 50.1 us -> 48.8 us (0.974)
  Pallas kernels: 49.8 us -> 48.5 us
    pallas_call x1, Pallas kernels: 45.8 us -> 44.6 us  [local(): pl.pallas_call(step_kernel, out_shape=(jax.ShapeDtypeStruct((S, D), BF),...]
where the time goes in v4:
time: 48.8 us; the launch traced here: 48.6 us
  Pallas kernels  48.5 us (99%)
    pallas_call x1, Pallas kernels, local(): pl.pallas_call(step_kernel, out_shape=(jax.ShapeDtypeStruct((S, D), BF),...  44.6 us
    pallas_call x1, Pallas kernels, local(): pl.pallas_call(scatter_kernel, out_shape=jax.ShapeDtypeStruct((V, D), F32...  3.89 us

profile of v4, /device:TPU:0, one launch (start us, length us, event | category | flops | bytes accessed | tf_op | source)
XLA Modules:
  0.0 48.6 jit_solution(8137385416187167007)
XLA Ops:
  0.0 44.6 %link_step.1 = (bf16[1024,512]{1,0:T(8,128)(2,1)}, s32[8,8,128]{2,1,0:T(8,128)}, bf16[384,512]{1,0:T(8,128)(2,1)}, f32[2,64,512]{2,1,0:T(8,128)}) custom-call(bf16[1024,512]{1,0:T(8,128)(2,1)} %table_hbm.1, s32[8,128]{1,0:T(8,128)} %bitcast.8, s32[1,2048]{1,0:T(1,128)} %bitcast.5, s32[1,2048]{1,0:T(1,128)} %bitcast.6, s32[1,2048]{1,0:T(1,128)} %bitcast.7, ...), custom_call_target="tpu_custom_call" | custom-call | tf_op jit(solution)/shard_map/link_step/pallas_call | solution.py:430
  44.6 3.9 %scatter.1 = f32[1024,512]{1,0:T(8,128)} custom-call(bf16[1024,512]{1,0:T(8,128)(2,1)} %get-tuple-element.9.ret_hbm, s32[8,8,128]{2,1,0:T(8,128)} %get-tuple-element.10.asked_hbm, s32[1,128]{1,0:T(1,128)} %bitcast.10, bf16[384,512]{1,0:T(8,128)(2,1)} %get-tuple-element.11.rs2_hbm, f32[2,64,512]{2,1,0:T(8,128)} %get-tuple-element.12.part_hbm), custom_call_target="tpu_custom_call" | custom-call | tf_op jit(solution)/shard_map/scatter/pallas_call | solution.py:488

commit v5 on v4

--- a/solution.py
+++ b/solution.py
@@ -281,7 +281,7 @@
     for dx in (0, 1, 3, 2)[:3]:
         score(dx, far, True)
     lost = arrive((0, 1, 3, 2)[3], lost)
-    score((0, 1, 3, 2)[3], pl.ds(0, C), False)
+    score((0, 1, 3, 2)[3], far, False)
 
     ret_cp = []
     rs_cp = {}
@@ -338,17 +338,21 @@
 
     opposite(0)
     opposite(1)
-    slot_grads(2)
+    slot_grads(1)
+    slot_grads(3)
+    score(2, near, True)
     neighbours_early(0)
     neighbours_early(1)
-    slot_grads(1)
-    slot_grads(3)
+    slot_grads(2)
     neighbours_late(0)
     neighbours_late(1)
     own_group(0)
     own_group(1)
     slot_grads(0)
     own_cp = local_copy(gst.at[chunk(0, 0)], ret.at[chunk(0, 0)], out_sem.at[1])
+    for cps in (req_cp, ag1, ag2, slot_cp):
+        for cp in cps.values():
+            cp.wait_send()
 
     rs2_cp = []
     for half in range(2):
@@ -373,10 +377,7 @@
 
     for cp in (asked_cp, own_cp, part_cp):
         cp.wait()
-    for cps in (req_cp, ag1, ag2, slot_cp, rs_cp):
-        for cp in cps.values():
-            cp.wait_send()
-    for cp in ret_cp + rs2_cp:
+    for cp in list(rs_cp.values()) + ret_cp + rs2_cp:
         cp.wait_send()
 
 
@@ -398,6 +399,10 @@
         place = jnp.where((place >= 0) & (place < 256), place, 256).astype(F32).astype(BF)
         return jnp.where(line == place, jnp.ones((256, R), BF), jnp.zeros((256, R), BF))
 
+    hots = []
+    for t in range(4):
+        negs = hot(neg[...], t * 256)
+        hots.append(jnp.concatenate([hot(asked[p, :1, :], t * 256) for p in range(8)] + [negs, negs], axis=1))
     loads[3].wait()
     loads[4].wait()
     for half in range(2):
@@ -412,9 +417,7 @@
     stores = []
     for t in range(4):
         at = pl.ds(t * 256, 256)
-        negs = hot(neg[...], t * 256)
-        hots = jnp.concatenate([hot(asked[p, :1, :], t * 256) for p in range(8)] + [negs, negs], axis=1)
-        out[at, :] = nn(hots, ret[...])
+        out[at, :] = nn(hots[t], ret[...])
         cp = pltpu.make_async_copy(out.at[at], out_hbm.at[at], out_sem.at[t])
         cp.start()
         stores.append(cp)

time: 48.8 us -> 48.3 us (0.990)
  Pallas kernels: 48.5 us -> 48 us
    pallas_call x1, Pallas kernels: 44.6 us -> 44.1 us  [local(): pl.pallas_call(step_kernel, out_shape=(jax.ShapeDtypeStruct((S, D), BF),...]
where the time goes in v5:
time: 48.3 us; the launch traced here: 48.1 us
  Pallas kernels  48 us (99%)
    pallas_call x1, Pallas kernels, local(): pl.pallas_call(step_kernel, out_shape=(jax.ShapeDtypeStruct((S, D), BF),...  44.1 us
    pallas_call x1, Pallas kernels, local(): pl.pallas_call(scatter_kernel, out_shape=jax.ShapeDtypeStruct((V, D), F32...  3.89 us

profile of v5, /device:TPU:0, one launch (start us, length us, event | category | flops | bytes accessed | tf_op | source)
XLA Modules:
  0.0 48.1 jit_solution(16963978644730765661)
XLA Ops:
  0.0 44.1 %link_step.1 = (bf16[1024,512]{1,0:T(8,128)(2,1)}, s32[8,8,128]{2,1,0:T(8,128)}, bf16[384,512]{1,0:T(8,128)(2,1)}, f32[2,64,512]{2,1,0:T(8,128)}) custom-call(bf16[1024,512]{1,0:T(8,128)(2,1)} %table_hbm.1, s32[8,128]{1,0:T(8,128)} %bitcast.8, s32[1,2048]{1,0:T(1,128)} %bitcast.5, s32[1,2048]{1,0:T(1,128)} %bitcast.6, s32[1,2048]{1,0:T(1,128)} %bitcast.7, ...), custom_call_target="tpu_custom_call" | custom-call | tf_op jit(solution)/shard_map/link_step/pallas_call | solution.py:433
  44.1 3.9 %scatter.1 = f32[1024,512]{1,0:T(8,128)} custom-call(bf16[1024,512]{1,0:T(8,128)(2,1)} %get-tuple-element.9.ret_hbm, s32[8,8,128]{2,1,0:T(8,128)} %get-tuple-element.10.asked_hbm, s32[1,128]{1,0:T(1,128)} %bitcast.10, bf16[384,512]{1,0:T(8,128)(2,1)} %get-tuple-element.11.rs2_hbm, f32[2,64,512]{2,1,0:T(8,128)} %get-tuple-element.12.part_hbm), custom_call_target="tpu_custom_call" | custom-call | tf_op jit(solution)/shard_map/scatter/pallas_call | solution.py:491

commit v6 on v5

--- a/solution.py
+++ b/solution.py
@@ -176,10 +176,11 @@
 
     pl.loop(0, 4)(incidence)
 
-    for cp in req_cp.values():
-        cp.wait_recv()
     slot_cp = {}
     for dx in (1, 3, 2, 0):
+        for dc in range(2):
+            if (dx, dc) != (0, 0):
+                req_cp[(4 - dx) % 4, dc].wait_recv()
         hot = jnp.concatenate([onehot_rows(asked[dx * 2], V), onehot_rows(asked[dx * 2 + 1], V)], axis=0)
         rows_out = nn(hot, table[...]).astype(BF)
         if dx == 0:

time: 48.3 us -> 50.6 us (1.048); the launches traced: 48.1 us -> 49.7 us
  Pallas kernels: 48 us -> 49.5 us
    pallas_call x1, Pallas kernels: 44.1 us -> 45.6 us  [local(): pl.pallas_call(step_kernel, out_shape=(jax.ShapeDtypeStruct((S, D), BF),...]
where the time goes in v6:
time: 50.6 us; the launch traced here: 49.7 us
  Pallas kernels  49.5 us (98%)
    pallas_call x1, Pallas kernels, local(): pl.pallas_call(step_kernel, out_shape=(jax.ShapeDtypeStruct((S, D), BF),...  45.6 us
    pallas_call x1, Pallas kernels, local(): pl.pallas_call(scatter_kernel, out_shape=jax.ShapeDtypeStruct((V, D), F32...  3.9 us

profile of v6, /device:TPU:0, one launch (start us, length us, event | category | flops | bytes accessed | tf_op | source)
XLA Modules:
  0.0 49.7 jit_solution(18237342944899753859)
XLA Ops:
  0.0 45.6 %link_step.1 = (bf16[1024,512]{1,0:T(8,128)(2,1)}, s32[8,8,128]{2,1,0:T(8,128)}, bf16[384,512]{1,0:T(8,128)(2,1)}, f32[2,64,512]{2,1,0:T(8,128)}) custom-call(bf16[1024,512]{1,0:T(8,128)(2,1)} %table_hbm.1, s32[8,128]{1,0:T(8,128)} %bitcast.8, s32[1,2048]{1,0:T(1,128)} %bitcast.5, s32[1,2048]{1,0:T(1,128)} %bitcast.6, s32[1,2048]{1,0:T(1,128)} %bitcast.7, ...), custom_call_target="tpu_custom_call" | custom-call | tf_op jit(solution)/shard_map/link_step/pallas_call | solution.py:434
  45.6 3.9 %scatter.1 = f32[1024,512]{1,0:T(8,128)} custom-call(bf16[1024,512]{1,0:T(8,128)(2,1)} %get-tuple-element.9.ret_hbm, s32[8,8,128]{2,1,0:T(8,128)} %get-tuple-element.10.asked_hbm, s32[1,128]{1,0:T(1,128)} %bitcast.10, bf16[384,512]{1,0:T(8,128)(2,1)} %get-tuple-element.11.rs2_hbm, f32[2,64,512]{2,1,0:T(8,128)} %get-tuple-element.12.part_hbm), custom_call_target="tpu_custom_call" | custom-call | tf_op jit(solution)/shard_map/scatter/pallas_call | solution.py:492
